TPU v7x, 768 devices: a whole 4x8x12 slice. The times are simulated.
768 devices in a mesh: slab: 192 (over y, z, core), col: 4 (over x).
Axes of the slice: x: 4, y: 8, z: 12, core: 2. Of those that a mesh axis runs over, the one named last changes fastest.
Arguments:
- prolong: bfloat16 [384, 8, 6, 4096], P('slab', 'col'), may hold values from -1 to 1
- coupling: bfloat16 [384, 8, 6, 28672], P('slab', 'col'), may hold values from -0.75 to 0.75
- jacobi_scale: bfloat16 [384, 8, 6, 64], P('slab', 'col'), may hold values from 0.19921875 to 0.59765625
- owner: int32 [2304, 1], P(('slab', 'col')), may hold values from 0 to 3; in each aligned block of 3 rows (0 to 2, 3 to 5, ...) at most 2 rows name the same one
Outputs:
- coarse_rows: bfloat16 [6144, 64, 448], P(('slab', 'col'))
Inputs may be any that keep to these rules, and one draw needn't show every extreme that they name: Each device's 3 rows name every owner at most 2 times, and in some devices one owner exactly 2 times.
All inputs are finite; a program needn't handle non-finite values.
Results may differ from a plain program's by a relative error of at most 0.0061.
Values may be sent and summed in bfloat16 or wider, within the bound.
No kernel may reach another device: no remote copies, remote signals or barrier semaphores. Data moves between devices by JAX's collectives and lax.ppermute only.
A program may use at most 32 MiB of HBM per device.

v0:
```python
import jax
import jax.numpy as jnp
from jax import lax
from jax.sharding import PartitionSpec as P

OFFSETS = ((1, 1, 1), (1, 1, 0), (1, 1, 2), (1, 0, 1), (1, 2, 1), (0, 1, 1), (2, 1, 1))


def extended(cells, sides, width):
    for axis, dim in sides:
        count = lax.axis_size(axis)
        ends = count - 1
        head = lax.slice_in_dim(cells, 0, width, axis=dim)
        tail = lax.slice_in_dim(cells, cells.shape[dim] - width, cells.shape[dim], axis=dim)
        cells = jnp.concatenate(
            [
                lax.ppermute(tail, axis, [(i, (i + 1) % count) for i in range(ends)]),
                cells,
                lax.ppermute(head, axis, [((i + 1) % count, i) for i in range(ends)]),
            ],
            axis=dim,
        )
    return cells


def smooth(tentative, self_block, scaling):
    product = jnp.einsum(
        "zyxij,zyxjk->zyxik", self_block, tentative, preferred_element_type=jnp.float32
    )
    return (
        tentative.astype(jnp.float32) - scaling.astype(jnp.float32)[..., None] * product
    ).astype(jnp.bfloat16)


def coarse_blocks(padded, blocks, coarse_width):
    layers, across, length = (blocks.shape[0], blocks.shape[1], blocks.shape[2])
    own = padded[1:-1, 1:-1, 1:-1]
    coords = (
        lax.broadcasted_iota(jnp.int32, (layers, across, length), 2),
        lax.broadcasted_iota(jnp.int32, (layers, across, length), 1),
        lax.broadcasted_iota(jnp.int32, (layers, across, length), 0),
    )
    parts = []
    total_self = None
    for direction in range(7):
        off_z, off_y, off_x = OFFSETS[direction]
        neighbor = padded[off_z : off_z + layers, off_y : off_y + across, off_x : off_x + length]
        left = jnp.einsum(
            "zyxik,zyxij->zyxkj",
            own,
            blocks[:, :, :, direction],
            preferred_element_type=jnp.float32,
        ).astype(jnp.bfloat16)
        term = jnp.einsum("zyxkj,zyxjl->zyxkl", left, neighbor, preferred_element_type=jnp.float32)
        if direction == 0:
            total_self = term
        else:
            inside = (coords[(direction - 1) // 2] % 2 == direction % 2).astype(jnp.float32)[
                ..., None, None
            ]
            total_self = total_self + inside * term
            parts.append((1.0 - inside) * term)
    stacked = jnp.stack([total_self] + parts, axis=4)
    summed = stacked.reshape(
        layers // 2, 2, across // 2, 2, length // 2, 2, coarse_width, 7, coarse_width
    ).sum(axis=(1, 3, 5))
    return summed.reshape(
        layers // 2 * (across // 2) * (length // 2), coarse_width * 7 * coarse_width
    ).astype(jnp.bfloat16)


def body(prolong, coupling, jacobi_scale, owner):
    layers, across, length, fine_width = jacobi_scale.shape
    coarse_width = prolong.shape[3] // fine_width
    blocks = coupling.reshape(layers, across, length, 7, fine_width, fine_width)
    packed = jnp.concatenate(
        (prolong, coupling[..., : fine_width * fine_width], jacobi_scale), axis=3
    )
    grown = extended(packed, (("slab", 0), ("col", 1)), 1)
    prolong_cut = fine_width * coarse_width
    block_cut = prolong_cut + fine_width * fine_width
    padded = smooth(
        grown[..., :prolong_cut].reshape(layers + 2, across + 2, length, fine_width, coarse_width),
        grown[..., prolong_cut:block_cut].reshape(
            layers + 2, across + 2, length, fine_width, fine_width
        ),
        grown[..., block_cut:],
    )
    padded = jnp.pad(padded, ((0, 0), (0, 0), (1, 1), (0, 0), (0, 0)))
    rows = coarse_blocks(padded, blocks, coarse_width)
    col_count = lax.axis_size("col")
    aggregates = owner.shape[0]
    capacity = max(2, (aggregates + col_count - 1) // col_count + aggregates // (2 * col_count))
    target = owner[:, 0]
    hits = (target[:, None] == lax.broadcasted_iota(jnp.int32, (aggregates, col_count), 1)).astype(
        jnp.int32
    )
    rank = jnp.sum((jnp.cumsum(hits, axis=0) - hits) * hits, axis=1)
    slot_of = target * capacity + rank
    select = (
        slot_of[None, :] == lax.broadcasted_iota(jnp.int32, (col_count * capacity, aggregates), 0)
    ).astype(jnp.bfloat16)
    outgoing = jnp.dot(select, rows, preferred_element_type=jnp.float32).astype(jnp.bfloat16)
    outgoing = outgoing.reshape(col_count, capacity, coarse_width, 7 * coarse_width)
    incoming = lax.all_to_all(outgoing, "col", split_axis=0, concat_axis=0, tiled=True)
    return incoming.reshape(col_count * capacity, coarse_width, 7 * coarse_width)


def solution(mesh):
    in_specs = (
        P("slab", "col", None, None),
        P("slab", "col", None, None),
        P("slab", "col", None, None),
        P(("slab", "col"), None),
    )
    out_specs = P(("slab", "col"), None, None)
    return jax.shard_map(body, mesh=mesh, in_specs=in_specs, out_specs=out_specs, check_vma=False)
```

profile of v0, /device:TPU:56, one launch (start us, length us, event | category | flops | bytes accessed | tf_op | source)
XLA Modules:
  0.0 86.9 jit_solution(18121138720828937970)
XLA Ops:
  0.0 1.1 %copy_dynamic-update-slice_fusion.1 = bf16[2,2,6,8256]{3,2,1,0:T(8,128)(2,1)S(1)} fusion(bf16[2,2,6,4096]{3,1,2,0:T(2,128)(2,1)} %param.4), kind=kLoop, calls=%fused_computation.45 | loop fusion | bytes 458752
  1.1 1.1 %slice.72 = bf16[2,2,6,4096]{3,1,2,0:T(2,128)(2,1)S(1)} slice(bf16[2,2,6,28672]{3,1,2,0:T(2,128)(2,1)} %param.5), slice={[0:2], [0:2], [0:6], [0:4096]} | slice | bytes 393216 | tf_op jit(solution)/shard_map/slice | solution.py:77
  2.3 0.7 constant_dynamic-update-slice_fusion
  3.0 1.9 %collective-permute-start = (bf16[1,2,6,8256]{3,2,1,0:T(8,128)(2,1)S(1)}, bf16[1,2,6,8256]{3,2,1,0:T(8,128)(2,1)S(1)}, u32[]{:S(2)}, u32[]{:S(2)}) collective-permute-start(bf16[1,2,6,8256]{3,2,1,0:T(8,128)(2,1)S(1)} %get-tuple-element.14), channel_id=1, source_target_pairs={{0,4},{4,8},{8,12},{12,16},{16,20},{20,24},{24,28},{28,32},{32,36}... | collective-permute-start | bytes 594440 | tf_op jit(solution)/shard_map/ppermute | solution.py:17
  5.0 14.8 %collective-permute-start.1 = (bf16[1,2,6,8256]{3,2,1,0:T(8,128)(2,1)S(1)}, bf16[1,2,6,8256]{3,2,1,0:T(8,128)(2,1)S(1)}, u32[]{:S(2)}, u32[]{:S(2)}) collective-permute-start(bf16[1,2,6,8256]{3,2,1,0:T(8,128)(2,1)S(1)} %get-tuple-element.15), channel_id=1, source_target_pairs={{4,0},{8,4},{12,8},{16,12},{20,16},{24,20},{28,24},{32,28},{36,32}... | collective-permute-start | bytes 594440 | tf_op jit(solution)/shard_map/ppermute | solution.py:19
  19.8 0.7 broadcast_subtract_fusion
  20.5 0.7 compare_convert_fusion.3
  22.6 1.0 %collective-permute-done.1 = bf16[1,2,6,8256]{3,2,1,0:T(8,128)(2,1)S(1)} collective-permute-done((bf16[1,2,6,8256]{3,2,1,0:T(8,128)(2,1)S(1)}, bf16[1,2,6,8256]{3,2,1,0:T(8,128)(2,1)S(1)}, u32[]{:S(2)}, u32[]{:S(2)}) %collective-permute-start.1) | collective-permute-done | bytes 198176 | tf_op jit(solution)/shard_map/ppermute | solution.py:19
  24.0 1.1 %fusion.21 = (bf16[4,1,6,8256]{3,2,1,0:T(8,128)(2,1)}, bf16[4,1,6,8256]{3,2,1,0:T(8,128)(2,1)}) fusion(bf16[4,2,6,8256]{3,2,1,0:T(8,128)(2,1)S(1)} %pad_maximum_fusion.1), kind=kLoop, calls=%fused_computation.82 | loop fusion | bytes 1585152 | tf_op jit(solution)/shard_map/slice | solution.py:14
  25.1 4.2 %collective-permute-start.2 = (bf16[4,1,6,8256]{3,2,1,0:T(8,128)(2,1)}, bf16[4,1,6,8256]{3,2,1,0:T(8,128)(2,1)}, u32[]{:S(2)}, u32[]{:S(2)}) collective-permute-start(bf16[4,1,6,8256]{3,2,1,0:T(8,128)(2,1)} %get-tuple-element.12), channel_id=1, source_target_pairs={{0,1},{1,2},{2,3},{4,5},{5,6},{6,7},{8,9},{9,10},{10,11},{12,13},{... | collective-permute-start | bytes 1188872 | tf_op jit(solution)/shard_map/ppermute | solution.py:17
  29.2 1.3 %collective-permute-start.3 = (bf16[4,1,6,8256]{3,2,1,0:T(8,128)(2,1)}, bf16[4,1,6,8256]{3,2,1,0:T(8,128)(2,1)}, u32[]{:S(2)}, u32[]{:S(2)}) collective-permute-start(bf16[4,1,6,8256]{3,2,1,0:T(8,128)(2,1)} %get-tuple-element.13), channel_id=1, source_target_pairs={{1,0},{2,1},{3,2},{5,4},{6,5},{7,6},{9,8},{10,9},{11,10},{13,12},{... | collective-permute-start | bytes 1188872 | tf_op jit(solution)/shard_map/ppermute | solution.py:19
  31.1 3.5 %reshape.72 = bf16[2,2,6,7,64,64]{5,4,3,1,2,0:T(8,128)(2,1)S(1)} reshape(bf16[2,2,6,28672]{3,1,2,0:T(2,128)(2,1)} %param.5) | data formatting | bytes 2752512 | tf_op jit(solution)/shard_map/reshape | solution.py:75
  34.7 1.6 %fusion.20 = (bf16[2,2,6,1,64,64]{5,4,3,1,2,0:T(8,128)(2,1)}, bf16[2,2,6,1,64,64]{5,4,3,1,2,0:T(8,128)(2,1)}, bf16[2,2,6,1,64,64]{5,4,3,1,2,0:T(8,128)(2,1)}, bf...) fusion(bf16[2,2,6,7,64,64]{5,4,3,1,2,0:T(8,128)(2,1)S(1)} %resh, ...), kind=kLoop, calls=%fused_computation.81 | loop fusion | bytes 2752512 | tf_op jit(solution)/shard_map/slice | solution.py:51
  36.2 4.5 %collective-permute-done.3 = bf16[4,1,6,8256]{3,2,1,0:T(8,128)(2,1)} collective-permute-done((bf16[4,1,6,8256]{3,2,1,0:T(8,128)(2,1)}, bf16[4,1,6,8256]{3,2,1,0:T(8,128)(2,1)}, u32[]{:S(2)}, u32[]{:S(2)}) %collective-permute-start.3) | collective-permute-done | bytes 396320 | tf_op jit(solution)/shard_map/ppermute | solution.py:19
  40.7 2.2 %pad_maximum_fusion.2 = bf16[4,4,6,4096]{3,2,1,0:T(8,128)(2,1)} fusion(bf16[4,1,6,8256]{3,2,1,0:T(8,128)(2,1)} %collective-permute-done.3, bf16[4,1,6,8256]{3,2,1,0:T(8,128)(2,1)} %collective-permute-done.2, bf16[1,2,6,8256]{3,2,1,0:T(8,128)(2,1)S(1)} %copy-done.2, bf16[2,2,6,8256]{3,2,1,0:T(8,128)(2,1)S(1)} %constant_dynamic-update-slice_fusion, ...), kind=kLoop, calls=%fused_computation.19 | loop fusion | flops 3932160 | bytes 2371584 | tf_op jit(solution)/shard_map/slice | solution.py:84
  42.9 2.8 %reshape.75 = bf16[4,4,6,64,64]{4,3,2,1,0:T(8,128)(2,1)S(1)} reshape(bf16[4,4,6,4096]{3,2,1,0:T(8,128)(2,1)} %pad_maximum_fusion.2) | data formatting | bytes 1572864 | tf_op jit(solution)/shard_map/reshape | solution.py:84
  45.8 1.9 %pad_maximum_fusion = bf16[4,4,6,8256]{3,2,1,0:T(8,128)(2,1)S(1)} fusion(bf16[4,1,6,8256]{3,2,1,0:T(8,128)(2,1)} %collective-permute-done.3, bf16[1,2,6,8256]{3,2,1,0:T(8,128)(2,1)S(1)} %copy-done.3, bf16[2,2,6,8256]{3,2,1,0:T(8,128)(2,1)S(1)} %constant_dynamic-update-slice_fusion, bf16[1,2,6,8256]{3,2,1,0:T(8,128)(2,1)S(1)} %collective-permute-done, ...), kind=kLoop, calls=%fused_computation.2 | loop fusion | flops 3170304 | bytes 3170304 | tf_op jit(solution)/shard_map/concatenate | solution.py:15
  47.7 1.1 %slice.98 = bf16[4,4,6,4096]{3,2,1,0:T(8,128)(2,1)} slice(bf16[4,4,6,8256]{3,2,1,0:T(8,128)(2,1)S(1)} %pad_maximum_fusion), slice={[0:4], [0:4], [0:6], [0:4096]} | slice | bytes 1572864 | tf_op jit(solution)/shard_map/slice | solution.py:83
  48.8 3.6 %reshape.76 = bf16[4,4,6,64,64]{4,3,2,1,0:T(8,128)(2,1)} reshape(bf16[4,4,6,4096]{3,2,1,0:T(8,128)(2,1)} %slice.98) | data formatting | bytes 1572864 | tf_op jit(solution)/shard_map/reshape | solution.py:83
  52.4 0.8 maximum_convert_fusion
  53.9 1.1 %subtract_convert_fusion = bf16[4,4,6,64,64]{4,3,2,1,0:T(8,128)(2,1)S(1)} fusion(bf16[4,4,6,64,64]{4,3,2,1,0:T(8,128)(2,1)S(1)} %copy-done, f32[4,4,6,64]{3,2,1,0:T(8,128)S(1)} %maximum_convert_fusion, bf16[4,4,6,64,64]{4,3,2,1,0:T(8,128)(2,1)S(1)} %reshape.75), kind=kOutput, calls=%fused_computation.1 | convolution fusion | flops 51904512 | bytes 2383872 | tf_op jit(solution)/shard_map/zyxij,zyxjk->zyxik/dot_general | solution.py:27
  55.3 0.7 copy-done.9
  63.4 1.0 %constant_dynamic-update-slice_fusion.7 = f32[1,2,1,2,3,2,64,7,64]{8,6,5,4,3,1,7,2,0:T(8,128)} fusion(f32[1,2,1,2,3,2,64,1,64]{8,6,5,4,3,1,7,2,0:T(8,128)S(1)} %bitcast.56), kind=kLoop, calls=%fused_computation.54 | loop fusion | bytes 1179648
  64.4 1.0 %constant_dynamic-update-slice_fusion.6 = f32[1,2,1,2,3,2,64,7,64]{8,6,5,4,3,1,7,2,0:T(8,128)} fusion(f32[1,2,1,2,3,2,64,7,64]{8,6,5,4,3,1,7,2,0:T(8,128)} %constant_dynamic-update-slice_fusion.7, f32[1,2,1,2,3,2,64,1,64]{8,6,5,4,3,1,7,2,0:T(8,128)S(1)} %bitcast.50), kind=kLoop, calls=%fused_computation.53 | loop fusion | bytes 1179648
  65.4 1.0 %constant_dynamic-update-slice_fusion.5 = f32[1,2,1,2,3,2,64,7,64]{8,6,5,4,3,1,7,2,0:T(8,128)} fusion(f32[1,2,1,2,3,2,64,7,64]{8,6,5,4,3,1,7,2,0:T(8,128)} %constant_dynamic-update-slice_fusion.6, f32[1,2,1,2,3,2,64,1,64]{8,6,5,4,3,1,7,2,0:T(8,128)S(1)} %bitcast.51), kind=kLoop, calls=%fused_computation.52 | loop fusion | bytes 1179648
  66.4 1.0 %constant_dynamic-update-slice_fusion.4 = f32[1,2,1,2,3,2,64,7,64]{8,6,5,4,3,1,7,2,0:T(8,128)} fusion(f32[1,2,1,2,3,2,64,7,64]{8,6,5,4,3,1,7,2,0:T(8,128)} %constant_dynamic-update-slice_fusion.5, f32[1,2,1,2,3,2,64,1,64]{8,6,5,4,3,1,7,2,0:T(8,128)S(1)} %bitcast.52), kind=kLoop, calls=%fused_computation.51 | loop fusion | bytes 1179648
  67.3 1.0 %constant_dynamic-update-slice_fusion.3 = f32[1,2,1,2,3,2,64,7,64]{8,6,5,4,3,1,7,2,0:T(8,128)} fusion(f32[1,2,1,2,3,2,64,7,64]{8,6,5,4,3,1,7,2,0:T(8,128)} %constant_dynamic-update-slice_fusion.4, f32[1,2,1,2,3,2,64,1,64]{8,6,5,4,3,1,7,2,0:T(8,128)S(1)} %bitcast.53), kind=kLoop, calls=%fused_computation.50 | loop fusion | bytes 1179648
  68.3 1.0 %constant_dynamic-update-slice_fusion.2 = f32[1,2,1,2,3,2,64,7,64]{8,6,5,4,3,1,7,2,0:T(8,128)} fusion(f32[1,2,1,2,3,2,64,7,64]{8,6,5,4,3,1,7,2,0:T(8,128)} %constant_dynamic-update-slice_fusion.3, f32[1,2,1,2,3,2,64,1,64]{8,6,5,4,3,1,7,2,0:T(8,128)S(1)} %bitcast.54), kind=kLoop, calls=%fused_computation.49 | loop fusion | bytes 1179648
  69.3 1.0 %constant_dynamic-update-slice_fusion.1 = f32[1,2,1,2,3,2,64,7,64]{8,6,5,4,3,1,7,2,0:T(8,128)} fusion(f32[1,2,1,2,3,2,64,7,64]{8,6,5,4,3,1,7,2,0:T(8,128)} %constant_dynamic-update-slice_fusion.2, f32[1,2,1,2,3,2,64,1,64]{8,6,5,4,3,1,7,2,0:T(8,128)S(1)} %bitcast.55), kind=kLoop, calls=%fused_computation.48 | loop fusion | bytes 1179648 | tf_op jit(solution)/shard_map/stack | solution.py:63
  70.3 3.2 %reduce_sum.19 = bf16[3,64,7,64]{3,1,0,2:T(8,128)(2,1)S(1)} reduce(f32[1,2,1,2,3,2,64,7,64]{8,6,5,4,3,1,7,2,0:T(8,128)} %constant_dynamic-update-slice_fusion.1, f32[]{:T(128)} %constant.47.clone.1), dimensions={0,1,2,3,5}, to_apply=%region_2.3 | reduce | flops 602112 | bytes 2924548 | tf_op jit(solution)/shard_map/reduce_sum | solution.py:66
  75.0 11.1 %all_to_all.5 = bf16[4,2,64,448]{3,2,1,0:T(8,128)(2,1)S(1)} all-to-all(bf16[4,2,64,448]{3,2,1,0:T(8,128)(2,1)S(1)} %reshape.73), channel_id=1, replica_groups=mesh['slab'=192,'col'=4] {'col'}, dimensions={0} | all-to-all | bytes 917504 | tf_op jit(solution)/shard_map/all_to_all | solution.py:105
  86.1 0.8 copy.117
  (80 shorter events, 12.1 us)
Async XLA Ops:
  0.0 21.2 %copy-start.22 = (s32[3,1]{0,1:T(1,128)S(1)}, s32[3,1]{0,1:T(1,128)}, u32[]{:S(2)}) copy-start(s32[3,1]{0,1:T(1,128)} %param.7) | copy-start | bytes 40
  3.0 19.6 %collective-permute-start = (bf16[1,2,6,8256]{3,2,1,0:T(8,128)(2,1)S(1)}, bf16[1,2,6,8256]{3,2,1,0:T(8,128)(2,1)S(1)}, u32[]{:S(2)}, u32[]{:S(2)}) collective-permute-start(bf16[1,2,6,8256]{3,2,1,0:T(8,128)(2,1)S(1)} %get-tuple-element.14), channel_id=1, source_target_pairs={{0,4},{4,8},{8,12},{12,16},{16,20},{20,24},{24,28},{28,32},{32,36}... | collective-permute-start | bytes 594440 | tf_op jit(solution)/shard_map/ppermute | solution.py:17
  5.0 18.7 %collective-permute-start.1 = (bf16[1,2,6,8256]{3,2,1,0:T(8,128)(2,1)S(1)}, bf16[1,2,6,8256]{3,2,1,0:T(8,128)(2,1)S(1)}, u32[]{:S(2)}, u32[]{:S(2)}) collective-permute-start(bf16[1,2,6,8256]{3,2,1,0:T(8,128)(2,1)S(1)} %get-tuple-element.15), channel_id=1, source_target_pairs={{4,0},{8,4},{12,8},{16,12},{20,16},{24,20},{28,24},{32,28},{36,32}... | collective-permute-start | bytes 594440 | tf_op jit(solution)/shard_map/ppermute | solution.py:19
  23.7 1.4 %copy-start.1 = (bf16[1,2,6,8256]{3,2,1,0:T(8,128)(2,1)}, bf16[1,2,6,8256]{3,2,1,0:T(8,128)(2,1)S(1)}, u32[]{:S(2)}) copy-start(bf16[1,2,6,8256]{3,2,1,0:T(8,128)(2,1)S(1)} %collective-permute-done.1) | copy-start | bytes 594436
  25.1 11.2 %collective-permute-start.2 = (bf16[4,1,6,8256]{3,2,1,0:T(8,128)(2,1)}, bf16[4,1,6,8256]{3,2,1,0:T(8,128)(2,1)}, u32[]{:S(2)}, u32[]{:S(2)}) collective-permute-start(bf16[4,1,6,8256]{3,2,1,0:T(8,128)(2,1)} %get-tuple-element.12), channel_id=1, source_target_pairs={{0,1},{1,2},{2,3},{4,5},{5,6},{6,7},{8,9},{9,10},{10,11},{12,13},{... | collective-permute-start | bytes 1188872 | tf_op jit(solution)/shard_map/ppermute | solution.py:17
  29.2 11.5 %collective-permute-start.3 = (bf16[4,1,6,8256]{3,2,1,0:T(8,128)(2,1)}, bf16[4,1,6,8256]{3,2,1,0:T(8,128)(2,1)}, u32[]{:S(2)}, u32[]{:S(2)}) collective-permute-start(bf16[4,1,6,8256]{3,2,1,0:T(8,128)(2,1)} %get-tuple-element.13), channel_id=1, source_target_pairs={{1,0},{2,1},{3,2},{5,4},{6,5},{7,6},{9,8},{10,9},{11,10},{13,12},{... | collective-permute-start | bytes 1188872 | tf_op jit(solution)/shard_map/ppermute | solution.py:19
  34.6 6.1 %copy-start.2 = (bf16[1,2,6,8256]{3,2,1,0:T(8,128)(2,1)S(1)}, bf16[1,2,6,8256]{3,2,1,0:T(8,128)(2,1)}, u32[]{:S(2)}) copy-start(bf16[1,2,6,8256]{3,2,1,0:T(8,128)(2,1)} %copy-done.1) | copy-start | bytes 594436
  42.9 2.9 %copy-start.3 = (bf16[1,2,6,8256]{3,2,1,0:T(8,128)(2,1)S(1)}, bf16[1,2,6,8256]{3,2,1,0:T(8,128)(2,1)}, u32[]{:S(2)}) copy-start(bf16[1,2,6,8256]{3,2,1,0:T(8,128)(2,1)} %copy-done.1) | copy-start | bytes 594436
  52.4 1.4 %copy-start = (bf16[4,4,6,64,64]{4,3,2,1,0:T(8,128)(2,1)S(1)}, bf16[4,4,6,64,64]{4,3,2,1,0:T(8,128)(2,1)}, u32[]{:S(2)}) copy-start(bf16[4,4,6,64,64]{4,3,2,1,0:T(8,128)(2,1)} %reshape.76) | copy-start | bytes 2359300
  53.9 1.1 %copy-start.10 = (bf16[2,2,6,1,64,64]{5,4,3,1,2,0:T(8,128)(2,1)S(1)}, bf16[2,2,6,1,64,64]{5,4,3,1,2,0:T(8,128)(2,1)}, u32[]{:S(2)}) copy-start(bf16[2,2,6,1,64,64]{5,4,3,1,2,0:T(8,128)(2,1)} %get-tuple-element.5) | copy-start | bytes 589828
  55.0 1.0 %copy-start.9 = (bf16[2,2,6,1,64,64]{5,4,3,1,2,0:T(8,128)(2,1)S(1)}, bf16[2,2,6,1,64,64]{5,4,3,1,2,0:T(8,128)(2,1)}, u32[]{:S(2)}) copy-start(bf16[2,2,6,1,64,64]{5,4,3,1,2,0:T(8,128)(2,1)} %get-tuple-element.9) | copy-start | bytes 589828
  55.3 1.0 %copy-start.8 = (bf16[2,2,6,1,64,64]{5,4,3,1,2,0:T(8,128)(2,1)S(1)}, bf16[2,2,6,1,64,64]{5,4,3,1,2,0:T(8,128)(2,1)}, u32[]{:S(2)}) copy-start(bf16[2,2,6,1,64,64]{5,4,3,1,2,0:T(8,128)(2,1)} %get-tuple-element.8) | copy-start | bytes 589828
  56.3 1.0 %copy-start.7 = (bf16[2,2,6,1,64,64]{5,4,3,1,2,0:T(8,128)(2,1)S(1)}, bf16[2,2,6,1,64,64]{5,4,3,1,2,0:T(8,128)(2,1)}, u32[]{:S(2)}) copy-start(bf16[2,2,6,1,64,64]{5,4,3,1,2,0:T(8,128)(2,1)} %get-tuple-element.7) | copy-start | bytes 589828
  56.6 1.0 %copy-start.6 = (bf16[2,2,6,1,64,64]{5,4,3,1,2,0:T(8,128)(2,1)S(1)}, bf16[2,2,6,1,64,64]{5,4,3,1,2,0:T(8,128)(2,1)}, u32[]{:S(2)}) copy-start(bf16[2,2,6,1,64,64]{5,4,3,1,2,0:T(8,128)(2,1)} %get-tuple-element.6) | copy-start | bytes 589828
  57.6 1.0 %copy-start.5 = (bf16[2,2,6,1,64,64]{5,4,3,1,2,0:T(8,128)(2,1)S(1)}, bf16[2,2,6,1,64,64]{5,4,3,1,2,0:T(8,128)(2,1)}, u32[]{:S(2)}) copy-start(bf16[2,2,6,1,64,64]{5,4,3,1,2,0:T(8,128)(2,1)} %get-tuple-element.11) | copy-start | bytes 589828
  58.0 1.0 %copy-start.4 = (bf16[2,2,6,1,64,64]{5,4,3,1,2,0:T(8,128)(2,1)S(1)}, bf16[2,2,6,1,64,64]{5,4,3,1,2,0:T(8,128)(2,1)}, u32[]{:S(2)}) copy-start(bf16[2,2,6,1,64,64]{5,4,3,1,2,0:T(8,128)(2,1)} %get-tuple-element.10) | copy-start | bytes 589828
  58.9 0.7 copy-start.17
  59.6 0.6 copy-start.16
  60.2 0.7 copy-start.21
  60.5 0.7 copy-start.20
  61.2 0.7 copy-start.19
  61.5 0.7 copy-start.18
  62.1 0.7 copy-start.11
  62.1 0.7 copy-start.12
  62.2 0.7 copy-start.13
  62.2 0.7 copy-start.14
  62.2 0.7 copy-start.15
  70.3 3.8 %copy-start.23 = (s32[3]{0:T(128)S(1)}, s32[3]{0:T(128)}, u32[]{:S(2)}) copy-start(s32[3]{0:T(128)} %multiply_add_fusion) | copy-start | bytes 40
where the time goes:
time: 87.6 us; the launch traced here: 86.9 us
  local copies, waits for them, and re-layouts  30.1 us (34%)
  starting transfers between devices  22.2 us (25%)
  other arithmetic  11.9 us (14%)
  blocking collectives  11.1 us (13%)
  matrix products  5.56 us (6%)
  waiting for transfers between devices  5.53 us (6%)
    ppermute x2, starting transfers between devices, extended(): lax.ppermute(head, axis, [((i + 1) % count, i) for i in range(ends)])  16.1 us
    unnamed x57, local copies, waits for them, and re-layouts  12.4 us
    all_to_all x1, blocking collectives, body(): lax.all_to_all(outgoing, 'col', split_axis=0, concat_axis=0, tiled=True)  11.1 us
    ppermute x2, starting transfers between devices, extended(): lax.ppermute(tail, axis, [(i, (i + 1) % count) for i in range(ends)])  6.1 us
    ppermute x2, waiting for transfers between devices, extended(): lax.ppermute(head, axis, [((i + 1) % count, i) for i in range(ends)])  5.52 us
    reshape x1, local copies, waits for them, and re-layouts, body(): grown[..., :prolong_cut]  3.61 us
    reshape x1, local copies, waits for them, and re-layouts, body(): blocks = coupling.reshape(layers, across, length, 7, fine_width, fine_width)  3.51 us
    reduce_sum x1, other arithmetic, coarse_blocks(): summed = stacked.reshape(layers // 2, 2, across // 2, 2, length // 2, 2,...  3.24 us
  transfers between devices with their start and end apart: 4, of which 2 were waited for; matrix products, arithmetic and copies ran while one was open for 10% of the time, Pallas kernels for 0%

commit v1 on v0

v1 whole, which is shorter than its diff:
```python
import functools

import jax
import jax.numpy as jnp
from jax import lax
from jax.experimental import pallas as pl
from jax.experimental.pallas import tpu as pltpu
from jax.sharding import PartitionSpec as P

FD = 64
LX = 6
LZ = 2
F32 = jnp.float32
BF16 = jnp.bfloat16


def low_lanes(rows):
    return lax.broadcasted_iota(jnp.int32, (rows, 128), 1) < 64


def even_rows(rows):
    return lax.broadcasted_iota(jnp.int32, (rows, 128), 0) % 2 == 0


def swap_halves(block):
    return jnp.concatenate([block[:, 64:], block[:, :64]], axis=1)


def unpairing():
    row = lax.broadcasted_iota(jnp.int32, (128, 128), 0)
    col = lax.broadcasted_iota(jnp.int32, (128, 128), 1)
    same_y = row // 64 == col % 2
    same_i = row % 64 == (col % 64) // 2 * 2 + col // 64
    return (same_y & same_i).astype(F32).astype(BF16)


def doubled(paired, matrix):
    swapped = swap_halves(paired)
    low = low_lanes(64)
    stacked = jnp.concatenate([jnp.where(low, paired, swapped), jnp.where(low, swapped, paired)], axis=0)
    return jnp.dot(matrix, stacked, preferred_element_type=F32).astype(BF16)


def diagonal(twice):
    low = low_lanes(64)
    zero = jnp.zeros_like(twice)
    return jnp.concatenate([jnp.where(low, twice, zero), jnp.where(low, zero, twice)], axis=0)


def diagonal_of_packed(packed):
    low = low_lanes(32)
    swapped = swap_halves(packed)
    zero = jnp.zeros_like(packed)
    return jnp.concatenate(
        [
            jnp.where(low, packed, zero),
            jnp.where(low, swapped, zero),
            jnp.where(low, zero, swapped),
            jnp.where(low, zero, packed),
        ],
        axis=0,
    )


def pick_y(both):
    return jnp.where(even_rows(64), both[:, :128], both[:, 128:])


def smooth_kernel(p_ref, c_ref, s_ref, smooth_ref, twice_ref, zlo_ref, zhi_ref, ylo_ref, yhi_ref):
    pairs = LZ * LX
    rows = pairs * 64
    matrix = unpairing()
    row = lax.broadcasted_iota(jnp.int32, (rows, 2 * pairs), 0)
    col = lax.broadcasted_iota(jnp.int32, (rows, 2 * pairs), 1)
    picks = (col == row // 64 * 2 + row % 2).astype(F32).astype(BF16)
    spread = jnp.dot(picks, s_ref[...], preferred_element_type=F32)
    row = lax.broadcasted_iota(jnp.int32, (rows, 64), 0)
    col = lax.broadcasted_iota(jnp.int32, (rows, 64), 1)
    spread = jnp.where(row % 64 // 2 == col // 2, spread, 0.0).astype(BF16)
    row = lax.broadcasted_iota(jnp.int32, (64, 128), 0)
    col = lax.broadcasted_iota(jnp.int32, (64, 128), 1)
    halves = (row % 2 == col // 64).astype(F32).astype(BF16)
    scale = jnp.dot(spread, halves, preferred_element_type=F32)
    low = low_lanes(32)
    for z in range(LZ):
        for x in range(LX):
            n = z * LX + x
            tentative = p_ref[n * 64 : n * 64 + 64, :]
            twice = doubled(tentative, matrix)
            right = jnp.concatenate([diagonal(twice[:64]), diagonal(twice[64:])], axis=1)
            both = jnp.dot(c_ref[n, :64, :], right, preferred_element_type=F32)
            smoothed = (tentative.astype(F32) - scale[n * 64 : n * 64 + 64] * pick_y(both)).astype(BF16)
            smooth_ref[n * 64 : n * 64 + 64, :] = smoothed
            twice = doubled(smoothed, matrix)
            twice_ref[n] = twice
            for y in range(2):
                packed = jnp.where(low, twice[y * 64 : y * 64 + 32], twice[y * 64 + 32 : y * 64 + 64])
                at = (x * 2 + y) * 32
                (zlo_ref, zhi_ref)[z][at : at + 32, :] = packed
                at = n * 32
                (ylo_ref, yhi_ref)[y][at : at + 32, :] = packed


def combine(even, odd):
    low = low_lanes(64)
    return jnp.where(low, even[:64], odd[64:]) + swap_halves(jnp.where(low, odd[:64], even[64:]))


def transposed_dot(left, right):
    return lax.dot_general(left, right, (((0,), (0,)), ((), ())), preferred_element_type=F32)


def local_kernel(c_ref, smooth_ref, twice_ref, part_ref):
    def both_y(n, swapped=False):
        twice = twice_ref[n]
        first, second = diagonal(twice[:64]), diagonal(twice[64:])
        return jnp.concatenate([second, first] if swapped else [first, second], axis=1)

    even = even_rows(64)
    inner, outer = {}, {}
    for z in range(LZ):
        for x in range(LX):
            n = z * LX + x
            block = lambda d: c_ref[n, d * 64 : d * 64 + 64, :]
            across = jnp.where(even, block(4), block(3))
            left = jnp.concatenate([block(0), block(2 - x % 2), block(6 - z), across], axis=1)
            right = jnp.concatenate(
                [both_y(n), both_y(z * LX + (x ^ 1)), both_y((1 - z) * LX + x), both_y(n, True)], axis=0
            )
            inner[z, x] = pick_y(jnp.dot(left, right, preferred_element_type=F32)).astype(BF16)
            beside = x - 1 if x % 2 == 0 else x + 1
            if 0 <= beside < LX:
                outer[z, x] = pick_y(
                    jnp.dot(block(1 + x % 2), both_y(z * LX + beside), preferred_element_type=F32)
                ).astype(BF16)
    for a in range(LX // 2):
        own = {}
        for z in range(LZ):
            for x in (2 * a, 2 * a + 1):
                n = z * LX + x
                own[z, x] = smooth_ref[n * 64 : n * 64 + 64, :]
        order = [(z, x) for z in range(LZ) for x in (2 * a, 2 * a + 1)]
        total = transposed_dot(
            jnp.concatenate([own[k] for k in order], axis=0), jnp.concatenate([inner[k] for k in order], axis=0)
        )
        sides = []
        for x in (2 * a, 2 * a + 1):
            if (0, x) in outer:
                sides.append(
                    transposed_dot(
                        jnp.concatenate([own[0, x], own[1, x]], axis=0),
                        jnp.concatenate([outer[0, x], outer[1, x]], axis=0),
                    )
                )
            else:
                sides.append(jnp.zeros((128, 128), F32))
        part_ref[a, :, :128] = combine(total, sides[0]).astype(BF16)
        part_ref[a, :, 128:] = combine(sides[1], jnp.zeros((128, 128), F32)).astype(BF16)


def halo_kernel(owner_ref, c_ref, smooth_ref, part_ref, zlo_ref, zhi_ref, ylo_ref, yhi_ref, out_ref):
    even = even_rows(64)
    across, along = {}, {}
    for z in range(LZ):
        for x in range(LX):
            n = z * LX + x
            block = lambda d: c_ref[n, d * 64 : d * 64 + 64, :]
            right = jnp.concatenate(
                [diagonal_of_packed(ref[n * 32 : n * 32 + 32, :]) for ref in (ylo_ref, yhi_ref)], axis=1
            )
            left = jnp.where(even, block(3), block(4))
            across[z, x] = pick_y(jnp.dot(left, right, preferred_element_type=F32)).astype(BF16)
            ref = (zlo_ref, zhi_ref)[z]
            right = jnp.concatenate(
                [diagonal_of_packed(ref[(x * 2 + y) * 32 : (x * 2 + y) * 32 + 32, :]) for y in range(2)], axis=1
            )
            along[z, x] = pick_y(jnp.dot(block(5 + z), right, preferred_element_type=F32)).astype(BF16)
    out_ref[...] = jnp.zeros_like(out_ref)
    zero = jnp.zeros((64, 128), BF16)
    low = low_lanes(64)
    owners = [owner_ref[a, 0] for a in range(LX // 2)]
    for a in range(LX // 2):
        own = {}
        for z in range(LZ):
            for x in (2 * a, 2 * a + 1):
                n = z * LX + x
                own[z, x] = smooth_ref[n * 64 : n * 64 + 64, :]
        order = [(z, x) for z in range(LZ) for x in (2 * a, 2 * a + 1)]
        right = jnp.concatenate(
            [
                jnp.concatenate([jnp.where(even, across[k], zero), jnp.where(even, zero, across[k])], axis=1)
                for k in order
            ],
            axis=0,
        )
        sides = transposed_dot(jnp.concatenate([own[k] for k in order], axis=0), right)
        ends = [
            transposed_dot(
                jnp.concatenate([own[z, 2 * a], own[z, 2 * a + 1]], axis=0),
                jnp.concatenate([along[z, 2 * a], along[z, 2 * a + 1]], axis=0),
            )
            for z in range(LZ)
        ]
        rank = sum([(owners[b] == owners[a]).astype(jnp.int32) for b in range(a)], jnp.int32(0))
        slot = owners[a] * 2 + rank
        empty = jnp.zeros((128, 128), F32)
        out_ref[slot, :, 0:128] = part_ref[a, :, :128]
        second = combine(empty, sides[:, :128]).astype(BF16)
        out_ref[slot, :, 128:256] = jnp.where(low, part_ref[a, :, 128:], second)
        out_ref[slot, :, 256:384] = combine(sides[:, 128:], ends[0]).astype(BF16)
        out_ref[slot, :, 384:448] = combine(ends[1], empty).astype(BF16)[:, :64]


def vmem(count):
    return [pl.BlockSpec(memory_space=pltpu.VMEM)] * count


def paired(array):
    layers, across, length, width = array.shape
    lanes = array.transpose(0, 2, 1, 3).reshape(layers, length, across, width // 128, 128)
    return lanes.transpose(0, 1, 3, 2, 4)


def body(prolong, coupling, jacobi_scale, owner):
    tentative = paired(prolong).reshape(LZ * LX * 64, 128)
    blocks = paired(coupling).reshape(LZ * LX, 448, 128)
    scale = jacobi_scale.transpose(0, 2, 1, 3).reshape(LZ * LX * 2, 64)
    face = jax.ShapeDtypeStruct((LX * 2 * 32, 128), BF16)
    params = pltpu.CompilerParams(vmem_limit_bytes=40 * 2**20)
    smoothed, twice, zlo, zhi, ylo, yhi = pl.pallas_call(
        smooth_kernel,
        out_shape=(
            jax.ShapeDtypeStruct((LZ * LX * 64, 128), BF16),
            jax.ShapeDtypeStruct((LZ * LX, 128, 128), BF16),
            face,
            face,
            face,
            face,
        ),
        in_specs=vmem(3),
        out_specs=tuple(vmem(6)),
        compiler_params=params,
        name="smooth",
    )(tentative, blocks, scale)
    up = lambda a, axis: lax.ppermute(a, axis, [(i, i + 1) for i in range(lax.axis_size(axis) - 1)])
    down = lambda a, axis: lax.ppermute(a, axis, [(i + 1, i) for i in range(lax.axis_size(axis) - 1)])
    from_ylo, from_yhi = up(yhi, "col"), down(ylo, "col")
    from_zlo, from_zhi = up(zhi, "slab"), down(zlo, "slab")
    part = pl.pallas_call(
        local_kernel,
        out_shape=jax.ShapeDtypeStruct((LX // 2, 64, 256), BF16),
        in_specs=vmem(3),
        out_specs=vmem(1)[0],
        compiler_params=params,
        cost_estimate=pl.CostEstimate(flops=2 * 10**9, bytes_accessed=3 * 10**6, transcendentals=0),
        name="local_blocks",
    )(blocks, smoothed, twice)
    outgoing = pl.pallas_call(
        halo_kernel,
        out_shape=jax.ShapeDtypeStruct((8, 64, 448), BF16),
        in_specs=[pl.BlockSpec(memory_space=pltpu.SMEM)] + vmem(7),
        out_specs=vmem(1)[0],
        compiler_params=params,
        name="halo_blocks",
    )(owner, blocks, smoothed, part, from_zlo, from_zhi, from_ylo, from_yhi)
    incoming = lax.all_to_all(outgoing.reshape(4, 2, 64, 448), "col", split_axis=0, concat_axis=0, tiled=True)
    return incoming.reshape(8, 64, 448)


def solution(mesh):
    in_specs = (
        P("slab", "col", None, None),
        P("slab", "col", None, None),
        P("slab", "col", None, None),
        P(("slab", "col"), None),
    )
    out_specs = P(("slab", "col"), None, None)
    return jax.shard_map(body, mesh=mesh, in_specs=in_specs, out_specs=out_specs, check_vma=False)
```

time: 87.6 us -> 47 us (0.54)
  local copies, waits for them, and re-layouts: 30.1 us -> 3.86 us
  other arithmetic: 11.9 us -> 0 us
  matrix products: 5.56 us -> 0 us
  Pallas kernels: 0 us -> 5.35 us
  waiting for transfers between devices: 5.53 us -> 4.12 us
    reshape x4 -> x0, local copies, waits for them, and re-layouts: 10.6 us -> none  [the longest x1 3.61 us: body(): grown[..., :prolong_cut]]
    unnamed x57 -> x12, local copies, waits for them, and re-layouts: 12.4 us -> 3.86 us
    dot_general x16 -> x0, matrix products: 5.56 us -> none  [the longest x7 2.13 us: coarse_blocks(): jnp.einsum('zyxik,zyxij->zyxkj', own, blocks[:, :, :, direction], preferr...]
    pallas_call x0 -> x3, Pallas kernels: none -> 5.35 us  [the longest x1 3.14 us: body(): pl.pallas_call(smooth_kernel, out_shape=(jax.ShapeDtypeStruct((LZ * LX *...]
    slice x5 -> x0, local copies, waits for them, and re-layouts: 4.87 us -> none  [the longest x1 1.57 us: coarse_blocks(): blocks[:, :, :, direction]]
    reduce_sum x2 -> x0, other arithmetic: 3.42 us -> none  [the longest x1 3.24 us: coarse_blocks(): summed = stacked.reshape(layers // 2, 2, across // 2, 2, length // 2, 2,...]
    slice x1 -> x0, other arithmetic: 2.23 us -> none  [body(): grown[..., prolong_cut:block_cut]]
    concatenate x2 -> x0, other arithmetic: 2.21 us -> none  [extended(): jnp.concatenate([lax.ppermute(tail, axis, [(i, (i + 1) % count) for i in...]
  transfers between devices with their start and end apart: 4 -> 4, of which waited for: 2 -> 2; matrix products, arithmetic and copies ran while one was open for 10% -> 0% of each run, Pallas kernels for 0% -> 2%
where the time goes in v1:
time: 47 us; the launch traced here: 46.7 us
  starting transfers between devices  21.4 us (46%)
  blocking collectives  11.9 us (25%)
  Pallas kernels  5.35 us (11%)
  waiting for transfers between devices  4.12 us (9%)
  local copies, waits for them, and re-layouts  3.86 us (8%)
    ppermute x2, starting transfers between devices, body(): lax.ppermute(a, axis, [(i + 1, i) for i in range(lax.axis_size(axis) - 1)])  16.1 us
    all_to_all x1, blocking collectives, body(): lax.all_to_all(outgoing.reshape(4, 2, 64, 448), 'col', split_axis=0, conc...  11.9 us
    ppermute x2, starting transfers between devices, body(): lax.ppermute(a, axis, [(i, i + 1) for i in range(lax.axis_size(axis) - 1)])  5.32 us
    unnamed x12, local copies, waits for them, and re-layouts  3.86 us
    ppermute x2, waiting for transfers between devices, body(): lax.ppermute(a, axis, [(i + 1, i) for i in range(lax.axis_size(axis) - 1)])  3.35 us
    pallas_call x1, Pallas kernels, body(): pl.pallas_call(smooth_kernel, out_shape=(jax.ShapeDtypeStruct((LZ * LX *...  3.14 us
    pallas_call x1, Pallas kernels, body(): pl.pallas_call(halo_kernel, out_shape=jax.ShapeDtypeStruct((8, 64, 448),...  1.25 us
    pallas_call x1, Pallas kernels, body(): pl.pallas_call(local_kernel, out_shape=jax.ShapeDtypeStruct((LX // 2, 64,...  0.96 us
  transfers between devices with their start and end apart: 4, of which 2 were waited for; matrix products, arithmetic and copies ran while one was open for 0% of the time, Pallas kernels for 2%

profile of v1, /device:TPU:56, one launch (start us, length us, event | category | flops | bytes accessed | tf_op | source)
XLA Modules:
  0.0 46.7 jit_solution(9536006875737194307)
XLA Ops:
  0.0 0.0 copy-start.4
  0.0 0.0 copy-start
  0.0 1.4 %copy-done = bf16[2,2,6,28672]{3,1,2,0:T(2,128)(2,1)S(1)} copy-done((bf16[2,2,6,28672]{3,1,2,0:T(2,128)(2,1)S(1)}, bf16[2,2,6,28672]{3,1,2,0:T(2,128)(2,1)}, u32[]{:S(2)}) %copy-start) | copy-done | bytes 1376280
  1.4 0.0 copy-start.2
  1.4 0.9 %copy-done.2 = bf16[2,2,6,4096]{3,1,2,0:T(2,128)(2,1)S(1)} copy-done((bf16[2,2,6,4096]{3,1,2,0:T(2,128)(2,1)S(1)}, bf16[2,2,6,4096]{3,1,2,0:T(2,128)(2,1)}, u32[]{:S(2)}) %copy-start.2) | copy-done | bytes 196632
  2.3 0.0 copy-start.3
  2.3 0.7 %copy-done.3 = bf16[2,2,6,64]{3,1,2,0:T(2,128)(2,1)S(1)} copy-done((bf16[2,2,6,64]{3,1,2,0:T(2,128)(2,1)S(1)}, bf16[2,2,6,64]{3,1,2,0:T(2,128)(2,1)}, u32[]{:S(2)}) %copy-start.3) | copy-done | bytes 3096
  3.0 0.0 copy-start.1
  3.0 3.1 %smooth.1 = (bf16[768,128]{1,0:T(8,128)(2,1)S(1)}, bf16[12,128,128]{2,1,0:T(8,128)(2,1)S(1)}, bf16[384,128]{1,0:T(8,128)(2,1)S(1)}, bf16[384,128]{1,0:T(8,128)(2...) custom-call(bf16[768,128]{1,0:T(8,128)(2,1)S(1)} %bitcast.23, bf16[12,448,128]{2,1,0:T(8,128)(2,1)S(1)} %bitcast.19, ...), custom_call_target="tpu_custom_call" | custom-call | tf_op jit(solution)/shard_map/smooth/pallas_call | solution.py:230
  6.1 1.9 %collective-permute-start = (bf16[384,128]{1,0:T(8,128)(2,1)S(1)}, bf16[384,128]{1,0:T(8,128)(2,1)S(1)}, u32[]{:S(2)}, u32[]{:S(2)}) collective-permute-start(bf16[384,128]{1,0:T(8,128)(2,1)S(1)} %get-tuple-element.13), channel_id=1, source_target_pairs={{0,4},{4,8},{8,12},{12,16},{16,20},{20,24},{24,28},{28,32},{32,36}... | collective-permute-start | bytes 294920 | tf_op jit(solution)/shard_map/ppermute | solution.py:245
  8.1 14.8 %collective-permute-start.1 = (bf16[384,128]{1,0:T(8,128)(2,1)S(1)}, bf16[384,128]{1,0:T(8,128)(2,1)S(1)}, u32[]{:S(2)}, u32[]{:S(2)}) collective-permute-start(bf16[384,128]{1,0:T(8,128)(2,1)S(1)} %get-tuple-element.14), channel_id=1, source_target_pairs={{4,0},{8,4},{12,8},{16,12},{20,16},{24,20},{28,24},{32,28},{36,32}... | collective-permute-start | bytes 294920 | tf_op jit(solution)/shard_map/ppermute | solution.py:246
  22.9 3.4 %collective-permute-start.2 = (bf16[384,128]{1,0:T(8,128)(2,1)S(1)}, bf16[384,128]{1,0:T(8,128)(2,1)S(1)}, u32[]{:S(2)}, u32[]{:S(2)}) collective-permute-start(bf16[384,128]{1,0:T(8,128)(2,1)S(1)} %get-tuple-element.15), channel_id=1, source_target_pairs={{0,1},{1,2},{2,3},{4,5},{5,6},{6,7},{8,9},{9,10},{10,11},{12,13},{... | collective-permute-start | bytes 294920 | tf_op jit(solution)/shard_map/ppermute | solution.py:245
  26.3 1.3 %collective-permute-start.3 = (bf16[384,128]{1,0:T(8,128)(2,1)S(1)}, bf16[384,128]{1,0:T(8,128)(2,1)S(1)}, u32[]{:S(2)}, u32[]{:S(2)}) collective-permute-start(bf16[384,128]{1,0:T(8,128)(2,1)S(1)} %get-tuple-element.16), channel_id=1, source_target_pairs={{1,0},{2,1},{3,2},{5,4},{6,5},{7,6},{9,8},{10,9},{11,10},{13,12},{... | collective-permute-start | bytes 294920 | tf_op jit(solution)/shard_map/ppermute | solution.py:246
  27.6 0.0 copy-done.4
  27.6 0.1 copy.7.owner_ref
  27.7 0.0 copy-done.1
  27.7 1.0 %local_blocks.1.part_ref = bf16[3,64,256]{2,1,0:T(8,128)(2,1)S(1)} custom-call(bf16[12,448,128]{2,1,0:T(8,128)(2,1)S(1)} %bitcast.20, bf16[768,128]{1,0:T(8,128)(2,1)S(1)} %get-tuple-element.11.smooth_ref, bf16[12,128,128]{2,1,0:T(8,128)(2,1)S(1)} %get-tuple-element.12.twice_ref), custom_call_target="tpu_custom_call" | custom-call | flops 2000000000 | bytes 3000000 | tf_op jit(solution)/shard_map/local_blocks/pallas_call | solution.py:249
  28.6 0.0 collective-permute-done.zlo_ref
  28.7 0.0 collective-permute-done.1.zhi_ref
  28.7 0.8 %collective-permute-done.2.ylo_ref = bf16[384,128]{1,0:T(8,128)(2,1)S(1)} collective-permute-done((bf16[384,128]{1,0:T(8,128)(2,1)S(1)}, bf16[384,128]{1,0:T(8,128)(2,1)S(1)}, u32[]{:S(2)}, u32[]{:S(2)}) %collective-permute-start.2) | collective-permute-done | bytes 98336 | tf_op jit(solution)/shard_map/ppermute | solution.py:245
  29.4 3.3 %collective-permute-done.3.yhi_ref = bf16[384,128]{1,0:T(8,128)(2,1)S(1)} collective-permute-done((bf16[384,128]{1,0:T(8,128)(2,1)S(1)}, bf16[384,128]{1,0:T(8,128)(2,1)S(1)}, u32[]{:S(2)}, u32[]{:S(2)}) %collective-permute-start.3) | collective-permute-done | bytes 98336 | tf_op jit(solution)/shard_map/ppermute | solution.py:246
  32.8 1.3 %halo_blocks.1 = bf16[8,64,448]{2,1,0:T(8,128)(2,1)S(1)} custom-call(s32[3,1]{1,0:T(4,128)S(1)} %copy.7.owner_ref, bf16[12,448,128]{2,1,0:T(8,128)(2,1)S(1)} %bitcast.21, bf16[768,128]{1,0:T(8,128)(2,1)S(1)} %get-tuple-element.11.smooth_ref, bf16[3,64,256]{2,1,0:T(8,128)(2,1)S(1)} %local_blocks.1.part_ref, ...), custom_call_target="tpu_custom_call" | custom-call | tf_op jit(solution)/shard_map/halo_blocks/pallas_call | solution.py:258
  34.0 11.9 %all_to_all.5 = bf16[4,2,64,448]{3,2,1,0:T(8,128)(2,1)S(1)} all-to-all(bf16[4,2,64,448]{3,2,1,0:T(8,128)(2,1)S(1)} %bitcast.22), channel_id=1, replica_groups=mesh['slab'=192,'col'=4] {'col'}, dimensions={0} | all-to-all | bytes 917504 | tf_op jit(solution)/shard_map/all_to_all | solution.py:266
  45.9 0.8 %copy.9 = bf16[8,64,448]{2,1,0:T(8,128)(2,1)} copy(bf16[8,64,448]{2,1,0:T(8,128)(2,1)S(1)} %bitcast.25) | data formatting | bytes 917504
Async XLA Ops:
  0.0 27.6 %copy-start.4 = (s32[3,1]{0,1:T(1,128)S(1)}, s32[3,1]{0,1:T(1,128)}, u32[]{:S(2)}) copy-start(s32[3,1]{0,1:T(1,128)} %param.7) | copy-start | bytes 40
  0.0 1.4 %copy-start = (bf16[2,2,6,28672]{3,1,2,0:T(2,128)(2,1)S(1)}, bf16[2,2,6,28672]{3,1,2,0:T(2,128)(2,1)}, u32[]{:S(2)}) copy-start(bf16[2,2,6,28672]{3,1,2,0:T(2,128)(2,1)} %param.5) | copy-start | bytes 4128772
  1.4 0.9 %copy-start.2 = (bf16[2,2,6,4096]{3,1,2,0:T(2,128)(2,1)S(1)}, bf16[2,2,6,4096]{3,1,2,0:T(2,128)(2,1)}, u32[]{:S(2)}) copy-start(bf16[2,2,6,4096]{3,1,2,0:T(2,128)(2,1)} %param.4) | copy-start | bytes 589828
  2.3 0.7 %copy-start.3 = (bf16[2,2,6,64]{3,1,2,0:T(2,128)(2,1)S(1)}, bf16[2,2,6,64]{3,1,2,0:T(2,128)(2,1)}, u32[]{:S(2)}) copy-start(bf16[2,2,6,64]{3,1,2,0:T(2,128)(2,1)} %param.6) | copy-start | bytes 9220
  3.0 24.7 %copy-start.1 = (bf16[2,2,6,28672]{3,1,2,0:T(2,128)(2,1)S(1)}, bf16[2,2,6,28672]{3,1,2,0:T(2,128)(2,1)}, u32[]{:S(2)}) copy-start(bf16[2,2,6,28672]{3,1,2,0:T(2,128)(2,1)} %param.5) | copy-start | bytes 4128772
  6.1 22.5 %collective-permute-start = (bf16[384,128]{1,0:T(8,128)(2,1)S(1)}, bf16[384,128]{1,0:T(8,128)(2,1)S(1)}, u32[]{:S(2)}, u32[]{:S(2)}) collective-permute-start(bf16[384,128]{1,0:T(8,128)(2,1)S(1)} %get-tuple-element.13), channel_id=1, source_target_pairs={{0,4},{4,8},{8,12},{12,16},{16,20},{20,24},{24,28},{28,32},{32,36}... | collective-permute-start | bytes 294920 | tf_op jit(solution)/shard_map/ppermute | solution.py:245
  8.1 20.6 %collective-permute-start.1 = (bf16[384,128]{1,0:T(8,128)(2,1)S(1)}, bf16[384,128]{1,0:T(8,128)(2,1)S(1)}, u32[]{:S(2)}, u32[]{:S(2)}) collective-permute-start(bf16[384,128]{1,0:T(8,128)(2,1)S(1)} %get-tuple-element.14), channel_id=1, source_target_pairs={{4,0},{8,4},{12,8},{16,12},{20,16},{24,20},{28,24},{32,28},{36,32}... | collective-permute-start | bytes 294920 | tf_op jit(solution)/shard_map/ppermute | solution.py:246
  22.9 6.6 %collective-permute-start.2 = (bf16[384,128]{1,0:T(8,128)(2,1)S(1)}, bf16[384,128]{1,0:T(8,128)(2,1)S(1)}, u32[]{:S(2)}, u32[]{:S(2)}) collective-permute-start(bf16[384,128]{1,0:T(8,128)(2,1)S(1)} %get-tuple-element.15), channel_id=1, source_target_pairs={{0,1},{1,2},{2,3},{4,5},{5,6},{6,7},{8,9},{9,10},{10,11},{12,13},{... | collective-permute-start | bytes 294920 | tf_op jit(solution)/shard_map/ppermute | solution.py:245
  26.3 6.5 %collective-permute-start.3 = (bf16[384,128]{1,0:T(8,128)(2,1)S(1)}, bf16[384,128]{1,0:T(8,128)(2,1)S(1)}, u32[]{:S(2)}, u32[]{:S(2)}) collective-permute-start(bf16[384,128]{1,0:T(8,128)(2,1)S(1)} %get-tuple-element.16), channel_id=1, source_target_pairs={{1,0},{2,1},{3,2},{5,4},{6,5},{7,6},{9,8},{10,9},{11,10},{13,12},{... | collective-permute-start | bytes 294920 | tf_op jit(solution)/shard_map/ppermute | solution.py:246

commit v2 on v1

--- a/solution.py
+++ b/solution.py
@@ -1,5 +1,3 @@
-import functools
-
 import jax
 import jax.numpy as jnp
 from jax import lax
@@ -66,13 +64,11 @@
     return jnp.where(even_rows(64), both[:, :128], both[:, 128:])
 
 
-def smooth_kernel(p_ref, c_ref, s_ref, smooth_ref, twice_ref, zlo_ref, zhi_ref, ylo_ref, yhi_ref):
-    pairs = LZ * LX
-    rows = pairs * 64
-    matrix = unpairing()
-    row = lax.broadcasted_iota(jnp.int32, (rows, 2 * pairs), 0)
-    col = lax.broadcasted_iota(jnp.int32, (rows, 2 * pairs), 1)
-    picks = (col == row // 64 * 2 + row % 2).astype(F32).astype(BF16)
+def scales(s_ref, z):
+    rows = LX * 64
+    row = lax.broadcasted_iota(jnp.int32, (rows, 4 * LX), 0)
+    col = lax.broadcasted_iota(jnp.int32, (rows, 4 * LX), 1)
+    picks = (col == (row // 64 + z * LX) * 2 + row % 2).astype(F32).astype(BF16)
     spread = jnp.dot(picks, s_ref[...], preferred_element_type=F32)
     row = lax.broadcasted_iota(jnp.int32, (rows, 64), 0)
     col = lax.broadcasted_iota(jnp.int32, (rows, 64), 1)
@@ -80,25 +76,55 @@
     row = lax.broadcasted_iota(jnp.int32, (64, 128), 0)
     col = lax.broadcasted_iota(jnp.int32, (64, 128), 1)
     halves = (row % 2 == col // 64).astype(F32).astype(BF16)
-    scale = jnp.dot(spread, halves, preferred_element_type=F32)
+    return jnp.dot(spread, halves, preferred_element_type=F32)
+
+
+def smooth_kernel(
+    p_hbm, c_hbm, s_hbm, smooth_ref, twice_ref, zlo_ref, zhi_ref, ylo_ref, yhi_ref, p_ref, c_ref, s_ref, sems
+):
+    half = LX * 64
+    scaling = pltpu.make_async_copy(s_hbm, s_ref, sems.at[4])
+    scaling.start()
+    layers = []
+    for z in range(LZ):
+        layers.append(
+            (
+                pltpu.make_async_copy(
+                    p_hbm.at[z * half : z * half + half], p_ref.at[z * half : z * half + half], sems.at[2 * z]
+                ),
+                pltpu.make_async_copy(
+                    c_hbm.at[z * LX : z * LX + LX, 0:64], c_ref.at[z * LX : z * LX + LX], sems.at[2 * z + 1]
+                ),
+            )
+        )
+        for copy in layers[z]:
+            copy.start()
+    matrix = unpairing()
     low = low_lanes(32)
+    scaling.wait()
+    scale = [scales(s_ref, z) for z in range(LZ)]
     for z in range(LZ):
+        for copy in layers[z]:
+            copy.wait()
+        at = [z * half + x * 64 for x in range(LX)]
+        tentative = [p_ref[r : r + 64, :] for r in at]
+        twice = [doubled(block, matrix) for block in tentative]
+        right = [jnp.concatenate([diagonal(t[:64]), diagonal(t[64:])], axis=1) for t in twice]
+        both = [jnp.dot(c_ref[z * LX + x], right[x], preferred_element_type=F32) for x in range(LX)]
+        smoothed = [
+            (tentative[x].astype(F32) - scale[z][x * 64 : x * 64 + 64] * pick_y(both[x])).astype(BF16)
+            for x in range(LX)
+        ]
+        twice = [doubled(block, matrix) for block in smoothed]
         for x in range(LX):
-            n = z * LX + x
-            tentative = p_ref[n * 64 : n * 64 + 64, :]
-            twice = doubled(tentative, matrix)
-            right = jnp.concatenate([diagonal(twice[:64]), diagonal(twice[64:])], axis=1)
-            both = jnp.dot(c_ref[n, :64, :], right, preferred_element_type=F32)
-            smoothed = (tentative.astype(F32) - scale[n * 64 : n * 64 + 64] * pick_y(both)).astype(BF16)
-            smooth_ref[n * 64 : n * 64 + 64, :] = smoothed
-            twice = doubled(smoothed, matrix)
-            twice_ref[n] = twice
+            smooth_ref[at[x] : at[x] + 64, :] = smoothed[x]
+            twice_ref[z * LX + x] = twice[x]
             for y in range(2):
-                packed = jnp.where(low, twice[y * 64 : y * 64 + 32], twice[y * 64 + 32 : y * 64 + 64])
-                at = (x * 2 + y) * 32
-                (zlo_ref, zhi_ref)[z][at : at + 32, :] = packed
-                at = n * 32
-                (ylo_ref, yhi_ref)[y][at : at + 32, :] = packed
+                packed = jnp.where(low, twice[x][y * 64 : y * 64 + 32], twice[x][y * 64 + 32 : y * 64 + 64])
+                to = (x * 2 + y) * 32
+                (zlo_ref, zhi_ref)[z][to : to + 32, :] = packed
+                to = (z * LX + x) * 32
+                (ylo_ref, yhi_ref)[y][to : to + 32, :] = packed
 
 
 def combine(even, odd):
@@ -158,7 +184,7 @@
         part_ref[a, :, 128:] = combine(sides[1], jnp.zeros((128, 128), F32)).astype(BF16)
 
 
-def halo_kernel(owner_ref, c_ref, smooth_ref, part_ref, zlo_ref, zhi_ref, ylo_ref, yhi_ref, out_ref):
+def halo_kernel(owner_ref, c_ref, smooth_ref, part_ref, ylo_ref, yhi_ref, zlo_ref, zhi_ref, out_ref):
     even = even_rows(64)
     across, along = {}, {}
     for z in range(LZ):
@@ -204,11 +230,31 @@
         rank = sum([(owners[b] == owners[a]).astype(jnp.int32) for b in range(a)], jnp.int32(0))
         slot = owners[a] * 2 + rank
         empty = jnp.zeros((128, 128), F32)
-        out_ref[slot, :, 0:128] = part_ref[a, :, :128]
+        out_ref[slot, 0:64, :] = part_ref[a, :, :128]
         second = combine(empty, sides[:, :128]).astype(BF16)
-        out_ref[slot, :, 128:256] = jnp.where(low, part_ref[a, :, 128:], second)
-        out_ref[slot, :, 256:384] = combine(sides[:, 128:], ends[0]).astype(BF16)
-        out_ref[slot, :, 384:448] = combine(ends[1], empty).astype(BF16)[:, :64]
+        out_ref[slot, 64:128, :] = jnp.where(low, part_ref[a, :, 128:], second)
+        out_ref[slot, 128:192, :] = combine(sides[:, 128:], ends[0]).astype(BF16)
+        last = combine(ends[1], ends[1]).astype(BF16)
+        out_ref[slot, 192:224, :] = jnp.where(low[:32], last[:32], last[32:])
+
+
+def unpack_kernel(in_ref, out_hbm, last_ref, sems):
+    copies = [
+        pltpu.make_async_copy(
+            in_ref.at[:, p * 64 : p * 64 + 64, :], out_hbm.at[:, :, p * 128 : p * 128 + 128], sems.at[p]
+        )
+        for p in range(3)
+    ]
+    for copy in copies:
+        copy.start()
+    for slot in range(8):
+        packed = in_ref[slot, 192:224, :]
+        last_ref[slot, :32, :] = packed[:, :64]
+        last_ref[slot, 32:, :] = packed[:, 64:]
+    copies.append(pltpu.make_async_copy(last_ref, out_hbm.at[:, :, 384:448], sems.at[3]))
+    copies[3].start()
+    for copy in copies:
+        copy.wait()
 
 
 def vmem(count):
@@ -237,15 +283,21 @@
             face,
             face,
         ),
-        in_specs=vmem(3),
+        in_specs=[pl.BlockSpec(memory_space=pltpu.HBM)] * 3,
         out_specs=tuple(vmem(6)),
+        scratch_shapes=[
+            pltpu.VMEM((LZ * LX * 64, 128), BF16),
+            pltpu.VMEM((LZ * LX, 64, 128), BF16),
+            pltpu.VMEM((LZ * LX * 2, 64), BF16),
+            pltpu.SemaphoreType.DMA((5,)),
+        ],
         compiler_params=params,
         name="smooth",
-    )(tentative, blocks, scale)
+    )(*(pltpu.with_memory_space_constraint(a, pltpu.HBM) for a in (tentative, blocks, scale)))
     up = lambda a, axis: lax.ppermute(a, axis, [(i, i + 1) for i in range(lax.axis_size(axis) - 1)])
     down = lambda a, axis: lax.ppermute(a, axis, [(i + 1, i) for i in range(lax.axis_size(axis) - 1)])
+    from_zlo, from_zhi = up(zhi, "slab"), down(zlo, "slab")
     from_ylo, from_yhi = up(yhi, "col"), down(ylo, "col")
-    from_zlo, from_zhi = up(zhi, "slab"), down(zlo, "slab")
     part = pl.pallas_call(
         local_kernel,
         out_shape=jax.ShapeDtypeStruct((LX // 2, 64, 256), BF16),
@@ -257,14 +309,22 @@
     )(blocks, smoothed, twice)
     outgoing = pl.pallas_call(
         halo_kernel,
-        out_shape=jax.ShapeDtypeStruct((8, 64, 448), BF16),
+        out_shape=jax.ShapeDtypeStruct((8, 224, 128), BF16),
         in_specs=[pl.BlockSpec(memory_space=pltpu.SMEM)] + vmem(7),
         out_specs=vmem(1)[0],
         compiler_params=params,
         name="halo_blocks",
-    )(owner, blocks, smoothed, part, from_zlo, from_zhi, from_ylo, from_yhi)
-    incoming = lax.all_to_all(outgoing.reshape(4, 2, 64, 448), "col", split_axis=0, concat_axis=0, tiled=True)
-    return incoming.reshape(8, 64, 448)
+    )(owner, blocks, smoothed, part, from_ylo, from_yhi, from_zlo, from_zhi)
+    incoming = lax.all_to_all(outgoing.reshape(4, 448, 128), "col", split_axis=0, concat_axis=0, tiled=True)
+    return pl.pallas_call(
+        unpack_kernel,
+        out_shape=jax.ShapeDtypeStruct((8, 64, 448), BF16),
+        in_specs=vmem(1),
+        out_specs=pl.BlockSpec(memory_space=pltpu.HBM),
+        scratch_shapes=[pltpu.VMEM((8, 64, 64), BF16), pltpu.SemaphoreType.DMA((4,))],
+        compiler_params=params,
+        name="unpack",
+    )(incoming.reshape(8, 224, 128))
 
 
 def solution(mesh):

time: 47 us -> 40.9 us (0.87)
  local copies, waits for them, and re-layouts: 3.86 us -> 0.1 us
  waiting for transfers between devices: 4.12 us -> 1.1 us
  blocking collectives: 11.9 us -> 12.7 us
    unnamed x12 -> x5, local copies, waits for them, and re-layouts: 3.86 us -> 0.1 us
    ppermute x2, waiting for transfers between devices: 3.35 us -> 1.09 us  [body(): lax.ppermute(a, axis, [(i + 1, i) for i in range(lax.axis_size(axis) - 1)])]
    pallas_call x1 -> x2, Pallas kernels: 1.25 us -> 2.11 us  [the longest x1 1.29 us: body(): pl.pallas_call(halo_kernel, out_shape=jax.ShapeDtypeStruct((8, 224, 128),...]
    all_to_all x1, blocking collectives: 11.9 us -> 12.7 us  [body(): lax.all_to_all(outgoing.reshape(4, 448, 128), 'col', split_axis=0, concat...]
    ppermute x2, waiting for transfers between devices: 0.77 us -> 0.01 us  [body(): lax.ppermute(a, axis, [(i, i + 1) for i in range(lax.axis_size(axis) - 1)])]
    pallas_call x1, Pallas kernels: 3.14 us -> 2.52 us  [body(): pl.pallas_call(smooth_kernel, out_shape=(jax.ShapeDtypeStruct((LZ * LX *...]
  transfers between devices with their start and end apart: 4 -> 4, of which waited for: 2 -> 1; matrix products, arithmetic and copies ran while one was open for 0% -> 0% of each run, Pallas kernels for 2% -> 2%
where the time goes in v2:
time: 40.9 us; the launch traced here: 40.7 us
  starting transfers between devices  21.1 us (52%)
  blocking collectives  12.7 us (31%)
  Pallas kernels  5.59 us (14%)
  waiting for transfers between devices  1.1 us (3%)
    ppermute x2, starting transfers between devices, body(): lax.ppermute(a, axis, [(i + 1, i) for i in range(lax.axis_size(axis) - 1)])  15.8 us
    all_to_all x1, blocking collectives, body(): lax.all_to_all(outgoing.reshape(4, 448, 128), 'col', split_axis=0, concat...  12.7 us
    ppermute x2, starting transfers between devices, body(): lax.ppermute(a, axis, [(i, i + 1) for i in range(lax.axis_size(axis) - 1)])  5.31 us
    pallas_call x1, Pallas kernels, body(): pl.pallas_call(smooth_kernel, out_shape=(jax.ShapeDtypeStruct((LZ * LX *...  2.52 us
    pallas_call x1, Pallas kernels, body(): pl.pallas_call(halo_kernel, out_shape=jax.ShapeDtypeStruct((8, 224, 128),...  1.29 us
    ppermute x2, waiting for transfers between devices, body(): lax.ppermute(a, axis, [(i + 1, i) for i in range(lax.axis_size(axis) - 1)])  1.09 us
    pallas_call x1, Pallas kernels, body(): pl.pallas_call(local_kernel, out_shape=jax.ShapeDtypeStruct((LX // 2, 64,...  0.96 us
  transfers between devices with their start and end apart: 4, of which 1 were waited for; matrix products, arithmetic and copies ran while one was open for 0% of the time, Pallas kernels for 2%

profile of v2, /device:TPU:56, one launch (start us, length us, event | category | flops | bytes accessed | tf_op | source)
XLA Modules:
  0.0 40.7 jit_solution(15360348013689431599)
XLA Ops:
  0.0 0.0 copy-start
  0.0 0.0 copy-start.1
  0.0 2.5 %smooth.1 = (bf16[768,128]{1,0:T(8,128)(2,1)S(1)}, bf16[12,128,128]{2,1,0:T(8,128)(2,1)S(1)}, bf16[384,128]{1,0:T(8,128)(2,1)S(1)}, bf16[384,128]{1,0:T(8,128)(2...) custom-call(bf16[768,128]{1,0:T(8,128)(2,1)} %bitcast.24, bf16[12,448,128]{2,1,0:T(8,128)(2,1)} %bitcast.19, ...), custom_call_target="tpu_custom_call" | custom-call | tf_op jit(solution)/shard_map/smooth/pallas_call | solution.py:276
  2.5 3.4 %collective-permute-start = (bf16[384,128]{1,0:T(8,128)(2,1)S(1)}, bf16[384,128]{1,0:T(8,128)(2,1)S(1)}, u32[]{:S(2)}, u32[]{:S(2)}) collective-permute-start(bf16[384,128]{1,0:T(8,128)(2,1)S(1)} %get-tuple-element.13), channel_id=1, source_target_pairs={{0,1},{1,2},{2,3},{4,5},{5,6},{6,7},{8,9},{9,10},{10,11},{12,13},{... | collective-permute-start | bytes 294920 | tf_op jit(solution)/shard_map/ppermute | solution.py:297
  5.9 1.3 %collective-permute-start.1 = (bf16[384,128]{1,0:T(8,128)(2,1)S(1)}, bf16[384,128]{1,0:T(8,128)(2,1)S(1)}, u32[]{:S(2)}, u32[]{:S(2)}) collective-permute-start(bf16[384,128]{1,0:T(8,128)(2,1)S(1)} %get-tuple-element.14), channel_id=1, source_target_pairs={{1,0},{2,1},{3,2},{5,4},{6,5},{7,6},{9,8},{10,9},{11,10},{13,12},{... | collective-permute-start | bytes 294920 | tf_op jit(solution)/shard_map/ppermute | solution.py:298
  7.2 1.9 %collective-permute-start.2 = (bf16[384,128]{1,0:T(8,128)(2,1)S(1)}, bf16[384,128]{1,0:T(8,128)(2,1)S(1)}, u32[]{:S(2)}, u32[]{:S(2)}) collective-permute-start(bf16[384,128]{1,0:T(8,128)(2,1)S(1)} %get-tuple-element.15), channel_id=1, source_target_pairs={{0,4},{4,8},{8,12},{12,16},{16,20},{20,24},{24,28},{28,32},{32,36}... | collective-permute-start | bytes 294920 | tf_op jit(solution)/shard_map/ppermute | solution.py:297
  9.2 14.5 %collective-permute-start.3 = (bf16[384,128]{1,0:T(8,128)(2,1)S(1)}, bf16[384,128]{1,0:T(8,128)(2,1)S(1)}, u32[]{:S(2)}, u32[]{:S(2)}) collective-permute-start(bf16[384,128]{1,0:T(8,128)(2,1)S(1)} %get-tuple-element.16), channel_id=1, source_target_pairs={{4,0},{8,4},{12,8},{16,12},{20,16},{24,20},{28,24},{32,28},{36,32}... | collective-permute-start | bytes 294920 | tf_op jit(solution)/shard_map/ppermute | solution.py:298
  23.7 0.0 copy-done.1
  23.7 0.1 copy.7.owner_ref
  23.8 0.0 copy-done
  23.8 1.0 %local_blocks.1.part_ref = bf16[3,64,256]{2,1,0:T(8,128)(2,1)S(1)} custom-call(bf16[12,448,128]{2,1,0:T(8,128)(2,1)S(1)} %bitcast.20, bf16[768,128]{1,0:T(8,128)(2,1)S(1)} %get-tuple-element.11.smooth_ref, bf16[12,128,128]{2,1,0:T(8,128)(2,1)S(1)} %get-tuple-element.12.twice_ref), custom_call_target="tpu_custom_call" | custom-call | flops 2000000000 | bytes 3000000 | tf_op jit(solution)/shard_map/local_blocks/pallas_call | solution.py:301
  24.8 0.0 collective-permute-done.ylo_ref
  24.8 0.0 collective-permute-done.1.yhi_ref
  24.8 0.0 collective-permute-done.2.zlo_ref
  24.8 1.1 %collective-permute-done.3.zhi_ref = bf16[384,128]{1,0:T(8,128)(2,1)S(1)} collective-permute-done((bf16[384,128]{1,0:T(8,128)(2,1)S(1)}, bf16[384,128]{1,0:T(8,128)(2,1)S(1)}, u32[]{:S(2)}, u32[]{:S(2)}) %collective-permute-start.3) | collective-permute-done | bytes 98336 | tf_op jit(solution)/shard_map/ppermute | solution.py:298
  25.9 1.3 %halo_blocks.1 = bf16[8,224,128]{2,1,0:T(8,128)(2,1)S(1)} custom-call(s32[3,1]{1,0:T(4,128)S(1)} %copy.7.owner_ref, bf16[12,448,128]{2,1,0:T(8,128)(2,1)S(1)} %bitcast.21, bf16[768,128]{1,0:T(8,128)(2,1)S(1)} %get-tuple-element.11.smooth_ref, bf16[3,64,256]{2,1,0:T(8,128)(2,1)S(1)} %local_blocks.1.part_ref, ...), custom_call_target="tpu_custom_call" | custom-call | tf_op jit(solution)/shard_map/halo_blocks/pallas_call | solution.py:310
  27.2 12.7 %all_to_all.5 = bf16[4,448,128]{2,1,0:T(8,128)(2,1)S(1)} all-to-all(bf16[4,448,128]{2,1,0:T(8,128)(2,1)S(1)} %bitcast.23), channel_id=1, replica_groups=mesh['slab'=192,'col'=4] {'col'}, dimensions={0} | all-to-all | bytes 917504 | tf_op jit(solution)/shard_map/all_to_all | solution.py:318
  39.9 0.8 %unpack.1 = bf16[8,64,448]{2,1,0:T(8,128)(2,1)} custom-call(bf16[8,224,128]{2,1,0:T(8,128)(2,1)S(1)} %bitcast.22), custom_call_target="tpu_custom_call" | custom-call | tf_op jit(solution)/shard_map/unpack/pallas_call | solution.py:319
Async XLA Ops:
  0.0 23.8 %copy-start = (bf16[2,2,6,28672]{3,1,2,0:T(2,128)(2,1)S(1)}, bf16[2,2,6,28672]{3,1,2,0:T(2,128)(2,1)}, u32[]{:S(2)}) copy-start(bf16[2,2,6,28672]{3,1,2,0:T(2,128)(2,1)} %param.5) | copy-start | bytes 4128772
  0.0 23.7 %copy-start.1 = (s32[3,1]{0,1:T(1,128)S(1)}, s32[3,1]{0,1:T(1,128)}, u32[]{:S(2)}) copy-start(s32[3,1]{0,1:T(1,128)} %param.7) | copy-start | bytes 40
  2.5 22.2 %collective-permute-start = (bf16[384,128]{1,0:T(8,128)(2,1)S(1)}, bf16[384,128]{1,0:T(8,128)(2,1)S(1)}, u32[]{:S(2)}, u32[]{:S(2)}) collective-permute-start(bf16[384,128]{1,0:T(8,128)(2,1)S(1)} %get-tuple-element.13), channel_id=1, source_target_pairs={{0,1},{1,2},{2,3},{4,5},{5,6},{6,7},{8,9},{9,10},{10,11},{12,13},{... | collective-permute-start | bytes 294920 | tf_op jit(solution)/shard_map/ppermute | solution.py:297
  5.9 18.9 %collective-permute-start.1 = (bf16[384,128]{1,0:T(8,128)(2,1)S(1)}, bf16[384,128]{1,0:T(8,128)(2,1)S(1)}, u32[]{:S(2)}, u32[]{:S(2)}) collective-permute-start(bf16[384,128]{1,0:T(8,128)(2,1)S(1)} %get-tuple-element.14), channel_id=1, source_target_pairs={{1,0},{2,1},{3,2},{5,4},{6,5},{7,6},{9,8},{10,9},{11,10},{13,12},{... | collective-permute-start | bytes 294920 | tf_op jit(solution)/shard_map/ppermute | solution.py:298
  7.2 17.6 %collective-permute-start.2 = (bf16[384,128]{1,0:T(8,128)(2,1)S(1)}, bf16[384,128]{1,0:T(8,128)(2,1)S(1)}, u32[]{:S(2)}, u32[]{:S(2)}) collective-permute-start(bf16[384,128]{1,0:T(8,128)(2,1)S(1)} %get-tuple-element.15), channel_id=1, source_target_pairs={{0,4},{4,8},{8,12},{12,16},{16,20},{20,24},{24,28},{28,32},{32,36}... | collective-permute-start | bytes 294920 | tf_op jit(solution)/shard_map/ppermute | solution.py:297
  9.2 16.7 %collective-permute-start.3 = (bf16[384,128]{1,0:T(8,128)(2,1)S(1)}, bf16[384,128]{1,0:T(8,128)(2,1)S(1)}, u32[]{:S(2)}, u32[]{:S(2)}) collective-permute-start(bf16[384,128]{1,0:T(8,128)(2,1)S(1)} %get-tuple-element.16), channel_id=1, source_target_pairs={{4,0},{8,4},{12,8},{16,12},{20,16},{24,20},{28,24},{32,28},{36,32}... | collective-permute-start | bytes 294920 | tf_op jit(solution)/shard_map/ppermute | solution.py:298

commit v3 on v2

v3 whole, which is shorter than its diff:
```python
import jax
import jax.numpy as jnp
from jax import lax
from jax.experimental import pallas as pl
from jax.experimental.pallas import tpu as pltpu
from jax.sharding import PartitionSpec as P

FD = 64
LX = 6
LZ = 2
F32 = jnp.float32
BF16 = jnp.bfloat16


def low_lanes(rows):
    return lax.broadcasted_iota(jnp.int32, (rows, 128), 1) < 64


def even_rows(rows):
    return lax.broadcasted_iota(jnp.int32, (rows, 128), 0) % 2 == 0


def swap_halves(block):
    return jnp.concatenate([block[:, 64:], block[:, :64]], axis=1)


def unpairing():
    row = lax.broadcasted_iota(jnp.int32, (128, 128), 0)
    col = lax.broadcasted_iota(jnp.int32, (128, 128), 1)
    same_y = row // 64 == col % 2
    same_i = row % 64 == (col % 64) // 2 * 2 + col // 64
    return (same_y & same_i).astype(F32).astype(BF16)


def doubled(blocks, matrix):
    low = low_lanes(64)
    stacked = []
    for paired in blocks:
        swapped = swap_halves(paired)
        stacked.append(jnp.concatenate([jnp.where(low, paired, swapped), jnp.where(low, swapped, paired)], axis=0))
    out = jnp.dot(matrix, jnp.concatenate(stacked, axis=1), preferred_element_type=F32).astype(BF16)
    return [out[:, n * 128 : n * 128 + 128] for n in range(len(blocks))]


def diagonal(twice):
    low = low_lanes(64)
    zero = jnp.zeros_like(twice)
    return jnp.concatenate([jnp.where(low, twice, zero), jnp.where(low, zero, twice)], axis=0)


def diagonal_of_packed(packed):
    low = low_lanes(32)
    swapped = swap_halves(packed)
    zero = jnp.zeros_like(packed)
    return jnp.concatenate(
        [
            jnp.where(low, packed, zero),
            jnp.where(low, swapped, zero),
            jnp.where(low, zero, swapped),
            jnp.where(low, zero, packed),
        ],
        axis=0,
    )


def pick_y(both):
    return jnp.where(even_rows(64), both[:, :128], both[:, 128:])


def scales(s_ref, z):
    rows = LX * 64
    row = lax.broadcasted_iota(jnp.int32, (rows, 4 * LX), 0)
    col = lax.broadcasted_iota(jnp.int32, (rows, 4 * LX), 1)
    picks = (col == (row // 64 + z * LX) * 2 + row % 2).astype(F32).astype(BF16)
    spread = jnp.dot(picks, s_ref[...], preferred_element_type=F32)
    row = lax.broadcasted_iota(jnp.int32, (rows, 64), 0)
    col = lax.broadcasted_iota(jnp.int32, (rows, 64), 1)
    spread = jnp.where(row % 64 // 2 == col // 2, spread, 0.0).astype(BF16)
    row = lax.broadcasted_iota(jnp.int32, (64, 128), 0)
    col = lax.broadcasted_iota(jnp.int32, (64, 128), 1)
    halves = (row % 2 == col // 64).astype(F32).astype(BF16)
    return jnp.dot(spread, halves, preferred_element_type=F32)


def smooth_kernel(
    p_hbm, c_hbm, s_hbm, o_hbm, smooth_ref, twice_ref, zlo_ref, zhi_ref, side_ref, p_ref, c_ref, d_ref, s_ref, o_ref, sems
):
    half = LX * 64
    scaling = pltpu.make_async_copy(s_hbm, s_ref, sems.at[6])
    naming = pltpu.make_async_copy(o_hbm, o_ref, sems.at[7])
    scaling.start()
    layers = []
    for z in range(LZ):
        rows, pairs = pl.ds(z * half, half), pl.ds(z * LX, LX)
        layers.append(
            (
                pltpu.make_async_copy(p_hbm.at[rows], p_ref.at[rows], sems.at[3 * z]),
                pltpu.make_async_copy(c_hbm.at[pairs, 0:64], c_ref.at[pairs], sems.at[3 * z + 1]),
                pltpu.make_async_copy(c_hbm.at[pairs, 192:256], d_ref.at[pairs], sems.at[3 * z + 2]),
            )
        )
        for copy in layers[z][:2]:
            copy.start()
    naming.start()
    for z in range(LZ):
        layers[z][2].start()
    matrix = unpairing()
    even = even_rows(64)
    low = low_lanes(32)
    zero = jnp.zeros((64, 128), BF16)
    scaling.wait()
    scale = [scales(s_ref, z) for z in range(LZ)]
    for z in range(LZ):
        for copy in layers[z][:2]:
            copy.wait()
        at = [z * half + x * 64 for x in range(LX)]
        tentative = [p_ref[r : r + 64, :] for r in at]
        twice = doubled(tentative, matrix)
        right = [jnp.concatenate([diagonal(t[:64]), diagonal(t[64:])], axis=1) for t in twice]
        both = [jnp.dot(c_ref[z * LX + x], right[x], preferred_element_type=F32) for x in range(LX)]
        smoothed = [
            (tentative[x].astype(F32) - scale[z][x * 64 : x * 64 + 64] * pick_y(both[x])).astype(BF16)
            for x in range(LX)
        ]
        twice = doubled(smoothed, matrix)
        layers[z][2].wait()
        left = [
            transposed_dot(jnp.where(even, d_ref[z * LX + x], zero), smoothed[x]) for x in range(LX)
        ]
        for x in range(0, LX, 2):
            to = (z * LX + x) * 32 + LZ * LX * 32
            side_ref[to : to + 64, :] = combine(left[x], left[x + 1]).astype(BF16)
        for x in range(LX):
            smooth_ref[at[x] : at[x] + 64, :] = smoothed[x]
            twice_ref[z * LX + x] = twice[x]
            for y in range(2):
                packed = jnp.where(low, twice[x][y * 64 : y * 64 + 32], twice[x][y * 64 + 32 : y * 64 + 64])
                to = (x * 2 + y) * 32
                (zlo_ref, zhi_ref)[z][to : to + 32, :] = packed
                if y == 0:
                    to = (z * LX + x) * 32
                    side_ref[to : to + 32, :] = packed
    naming.wait()
    owners = [jnp.broadcast_to(o_ref[:, a : a + 1], (16, 128)) for a in range(LX // 2)]
    for a in range(LX // 2):
        rank = sum([jnp.where(owners[b] == owners[a], 1, 0) for b in range(a)], jnp.zeros((16, 128), jnp.int32))
        slot = owners[a] * 2 + rank
        to = 2 * LZ * LX * 32 + a * 16
        side_ref[to : to + 16, :] = slot.astype(F32).astype(BF16)


def combine(even, odd):
    low = low_lanes(64)
    return jnp.where(low, even[:64], odd[64:]) + swap_halves(jnp.where(low, odd[:64], even[64:]))


def to_low(block):
    return block[:64] + swap_halves(block[64:])


def to_high(block):
    return swap_halves(block[:64]) + block[64:]


def transposed_dot(left, right):
    return lax.dot_general(left, right, (((0,), (0,)), ((), ())), preferred_element_type=F32)


def local_kernel(c_ref, smooth_ref, twice_ref, side_ref, part_ref, lent_ref):
    def both_y(n, swapped=False):
        twice = twice_ref[n]
        first, second = diagonal(twice[:64]), diagonal(twice[64:])
        return jnp.concatenate([second, first] if swapped else [first, second], axis=1)

    even = even_rows(64)
    zero = jnp.zeros((64, 128), BF16)
    inner, outer, across = {}, {}, {}
    for z in range(LZ):
        for x in range(LX):
            n = z * LX + x
            block = lambda d: c_ref[n, d * 64 : d * 64 + 64, :]
            mixed = jnp.where(even, block(4), block(3))
            left = jnp.concatenate([block(0), block(2 - x % 2), block(6 - z), mixed], axis=1)
            right = jnp.concatenate(
                [both_y(n), both_y(z * LX + (x ^ 1)), both_y((1 - z) * LX + x), both_y(n, True)], axis=0
            )
            inner[z, x] = pick_y(jnp.dot(left, right, preferred_element_type=F32)).astype(BF16)
            beside = x - 1 if x % 2 == 0 else x + 1
            if 0 <= beside < LX:
                outer[z, x] = pick_y(
                    jnp.dot(block(1 + x % 2), both_y(z * LX + beside), preferred_element_type=F32)
                ).astype(BF16)
            above = diagonal_of_packed(side_ref[n * 32 : n * 32 + 32, :])
            product = jnp.dot(block(4), above, preferred_element_type=F32).astype(BF16)
            across[z, x] = jnp.where(even, zero, product)
    for a in range(LX // 2):
        own = {}
        for z in range(LZ):
            for x in (2 * a, 2 * a + 1):
                n = z * LX + x
                own[z, x] = smooth_ref[n * 64 : n * 64 + 64, :]
        order = [(z, x) for z in range(LZ) for x in (2 * a, 2 * a + 1)]
        total = transposed_dot(
            jnp.concatenate([own[k] for k in order], axis=0),
            jnp.concatenate(
                [
                    jnp.concatenate([inner[k] for k in order], axis=0),
                    jnp.concatenate([across[k] for k in order], axis=0),
                ],
                axis=1,
            ),
        )
        sides = []
        for x in (2 * a, 2 * a + 1):
            if (0, x) in outer:
                sides.append(
                    transposed_dot(
                        jnp.concatenate([own[0, x], own[1, x]], axis=0),
                        jnp.concatenate([outer[0, x], outer[1, x]], axis=0),
                    )
                )
            else:
                sides.append(jnp.zeros((128, 128), F32))
        part_ref[a, 0:64, :] = combine(total[:, :128], sides[0]).astype(BF16)
        part_ref[a, 64:128, :] = to_low(total[:, 128:]).astype(BF16)
        part_ref[a, 128:192, :] = to_low(sides[1]).astype(BF16)
    low = low_lanes(32)
    lent = [jnp.zeros((32, 128), BF16)] * 8
    for a in range(LX // 2):
        begin = LZ * LX * 32
        left = jnp.concatenate(
            [side_ref[begin + (z * LX + 2 * a) * 32 : begin + (z * LX + 2 * a) * 32 + 64, :] for z in range(LZ)], axis=0
        )
        right = jnp.concatenate(
            [
                jnp.concatenate([twice_ref[z * LX + x, 64:, :] for z in range(LZ)], axis=0)
                for x in (2 * a, 2 * a + 1)
            ],
            axis=1,
        )
        product = transposed_dot(left, right)
        block = product[:64, :128] + product[64:, 128:]
        packed = jnp.where(low, block[:32], block[32:]).astype(BF16)
        slot = side_ref[2 * begin + a * 16 : 2 * begin + a * 16 + 16, :].astype(F32)
        slot = jnp.concatenate([slot, slot], axis=0)
        for place in range(8):
            lent[place] = jnp.where(slot == place, packed.astype(F32), lent[place].astype(F32)).astype(BF16)
    for place in range(8):
        lent_ref[place] = lent[place]


def halo_kernel(owner_ref, c_ref, smooth_ref, part_ref, lent_ref, zlo_ref, zhi_ref, out_ref):
    along = {}
    for z in range(LZ):
        for x in range(LX):
            n = z * LX + x
            ref = (zlo_ref, zhi_ref)[z]
            right = jnp.concatenate(
                [diagonal_of_packed(ref[(x * 2 + y) * 32 : (x * 2 + y) * 32 + 32, :]) for y in range(2)], axis=1
            )
            block = c_ref[n, (5 + z) * 64 : (6 + z) * 64, :]
            along[z, x] = pick_y(jnp.dot(block, right, preferred_element_type=F32)).astype(BF16)
    low = low_lanes(64)
    owners = [owner_ref[0, a] for a in range(LX // 2)]
    for place in range(8):
        out_ref[place, 0:192, :] = jnp.zeros((192, 128), BF16)
        out_ref[place, 192:224, :] = lent_ref[place]
    for a in range(LX // 2):
        ends = [
            to_high(
                transposed_dot(
                    jnp.concatenate(
                        [smooth_ref[(z * LX + x) * 64 : (z * LX + x) * 64 + 64, :] for x in (2 * a, 2 * a + 1)], axis=0
                    ),
                    jnp.concatenate([along[z, 2 * a], along[z, 2 * a + 1]], axis=0),
                )
            ).astype(BF16)
            for z in range(LZ)
        ]
        rank = sum([(owners[b] == owners[a]).astype(jnp.int32) for b in range(a)], jnp.int32(0))
        slot = owners[a] * 2 + rank
        out_ref[slot, 0:64, :] = part_ref[a, 0:64, :]
        out_ref[slot, 64:128, :] = jnp.where(low, part_ref[a, 64:128, :], ends[0])
        out_ref[slot, 128:192, :] = jnp.where(low, part_ref[a, 128:192, :], ends[1])


def unpack_kernel(in_ref, out_hbm, middle_ref, last_ref, sems):
    copies = [
        pltpu.make_async_copy(in_ref.at[:, 0:64, :], out_hbm.at[:, :, 0:128], sems.at[0]),
        pltpu.make_async_copy(in_ref.at[:, 64:128, :], out_hbm.at[:, :, 256:384], sems.at[1]),
    ]
    for copy in copies:
        copy.start()
    low = low_lanes(32)
    for slot in range(8):
        pair = in_ref[slot, 128:192, :]
        lent = in_ref[(slot + 6) % 8, 192:224, :]
        middle_ref[slot, :32, :] = jnp.where(low, pair[:32], swap_halves(lent))
        middle_ref[slot, 32:, :] = jnp.where(low, pair[32:], lent)
        last_ref[slot] = pair[:, 64:]
    copies.append(pltpu.make_async_copy(middle_ref, out_hbm.at[:, :, 128:256], sems.at[2]))
    copies.append(pltpu.make_async_copy(last_ref, out_hbm.at[:, :, 384:448], sems.at[3]))
    for copy in copies[2:]:
        copy.start()
    for copy in copies:
        copy.wait()


def vmem(count):
    return [pl.BlockSpec(memory_space=pltpu.VMEM)] * count


def paired(array):
    layers, across, length, width = array.shape
    lanes = array.transpose(0, 2, 1, 3).reshape(layers, length, across, width // 128, 128)
    return lanes.transpose(0, 1, 3, 2, 4)


def body(prolong, coupling, jacobi_scale, owner):
    tentative = paired(prolong).reshape(LZ * LX * 64, 128)
    blocks = paired(coupling).reshape(LZ * LX, 448, 128)
    scale = jacobi_scale.transpose(0, 2, 1, 3).reshape(LZ * LX * 2, 64)
    names = owner.T
    face = jax.ShapeDtypeStruct((LX * 2 * 32, 128), BF16)
    params = pltpu.CompilerParams(vmem_limit_bytes=40 * 2**20)
    arguments = (tentative, blocks, scale, names)
    smoothed, twice, zlo, zhi, side = pl.pallas_call(
        smooth_kernel,
        out_shape=(
            jax.ShapeDtypeStruct((LZ * LX * 64, 128), BF16),
            jax.ShapeDtypeStruct((LZ * LX, 128, 128), BF16),
            face,
            face,
            jax.ShapeDtypeStruct((2 * LZ * LX * 32 + 16 * (LX // 2), 128), BF16),
        ),
        in_specs=[pl.BlockSpec(memory_space=pltpu.HBM)] * 4,
        out_specs=tuple(vmem(5)),
        scratch_shapes=[
            pltpu.VMEM((LZ * LX * 64, 128), BF16),
            pltpu.VMEM((LZ * LX, 64, 128), BF16),
            pltpu.VMEM((LZ * LX, 64, 128), BF16),
            pltpu.VMEM((LZ * LX * 2, 64), BF16),
            pltpu.VMEM((1, LX // 2), jnp.int32),
            pltpu.SemaphoreType.DMA((8,)),
        ],
        compiler_params=params,
        name="smooth",
    )(*(pltpu.with_memory_space_constraint(a, pltpu.HBM) for a in arguments))
    up = lambda a, axis: lax.ppermute(a, axis, [(i, i + 1) for i in range(lax.axis_size(axis) - 1)])
    down = lambda a, axis: lax.ppermute(a, axis, [(i + 1, i) for i in range(lax.axis_size(axis) - 1)])
    from_zlo, from_zhi = up(zhi, "slab"), down(zlo, "slab")
    from_above = down(side, "col")
    part, lent = pl.pallas_call(
        local_kernel,
        out_shape=(
            jax.ShapeDtypeStruct((LX // 2, 192, 128), BF16),
            jax.ShapeDtypeStruct((8, 32, 128), BF16),
        ),
        in_specs=vmem(4),
        out_specs=tuple(vmem(2)),
        compiler_params=params,
        cost_estimate=pl.CostEstimate(flops=2 * 10**9, bytes_accessed=3 * 10**6, transcendentals=0),
        name="local_blocks",
    )(blocks, smoothed, twice, from_above)
    outgoing = pl.pallas_call(
        halo_kernel,
        out_shape=jax.ShapeDtypeStruct((8, 224, 128), BF16),
        in_specs=[pl.BlockSpec(memory_space=pltpu.SMEM)] + vmem(6),
        out_specs=vmem(1)[0],
        compiler_params=params,
        name="halo_blocks",
    )(names, blocks, smoothed, part, lent, from_zlo, from_zhi)
    incoming = lax.all_to_all(outgoing.reshape(4, 448, 128), "col", split_axis=0, concat_axis=0, tiled=True)
    return pl.pallas_call(
        unpack_kernel,
        out_shape=jax.ShapeDtypeStruct((8, 64, 448), BF16),
        in_specs=vmem(1),
        out_specs=pl.BlockSpec(memory_space=pltpu.HBM),
        scratch_shapes=[
            pltpu.VMEM((8, 64, 128), BF16),
            pltpu.VMEM((8, 64, 64), BF16),
            pltpu.SemaphoreType.DMA((4,)),
        ],
        compiler_params=params,
        name="unpack",
    )(incoming.reshape(8, 224, 128))


def solution(mesh):
    in_specs = (
        P("slab", "col", None, None),
        P("slab", "col", None, None),
        P("slab", "col", None, None),
        P(("slab", "col"), None),
    )
    out_specs = P(("slab", "col"), None, None)
    return jax.shard_map(body, mesh=mesh, in_specs=in_specs, out_specs=out_specs, check_vma=False)
```

time: 40.9 us -> 38.5 us (0.941)
  starting transfers between devices: 21.1 us -> 18 us
  Pallas kernels: 5.59 us -> 6.45 us
    ppermute x2 -> x1, starting transfers between devices: 5.31 us -> 1.92 us  [body(): lax.ppermute(a, axis, [(i, i + 1) for i in range(lax.axis_size(axis) - 1)])]
    pallas_call x1, Pallas kernels: 2.52 us -> 3.37 us  [body(): pl.pallas_call(smooth_kernel, out_shape=(jax.ShapeDtypeStruct((LZ * LX *...]
  transfers between devices with their start and end apart: 4 -> 3, of which waited for: 1 -> 1; matrix products, arithmetic and copies ran while one was open for 0% -> 0% of each run, Pallas kernels for 2% -> 3%
where the time goes in v3:
time: 38.5 us; the launch traced here: 38.3 us
  starting transfers between devices  18 us (47%)
  blocking collectives  12.7 us (33%)
  Pallas kernels  6.45 us (17%)
  waiting for transfers between devices  1.03 us (3%)
    ppermute x2, starting transfers between devices, body(): lax.ppermute(a, axis, [(i + 1, i) for i in range(lax.axis_size(axis) - 1)])  16.1 us
    all_to_all x1, blocking collectives, body(): lax.all_to_all(outgoing.reshape(4, 448, 128), 'col', split_axis=0, concat...  12.7 us
    pallas_call x1, Pallas kernels, body(): pl.pallas_call(smooth_kernel, out_shape=(jax.ShapeDtypeStruct((LZ * LX *...  3.37 us
    ppermute x1, starting transfers between devices, body(): lax.ppermute(a, axis, [(i, i + 1) for i in range(lax.axis_size(axis) - 1)])  1.92 us
    pallas_call x1, Pallas kernels, body(): pl.pallas_call(local_kernel, out_shape=(jax.ShapeDtypeStruct((LX // 2, 19...  1.11 us
    pallas_call x1, Pallas kernels, body(): pl.pallas_call(halo_kernel, out_shape=jax.ShapeDtypeStruct((8, 224, 128),...  1.11 us
    ppermute x2, waiting for transfers between devices, body(): lax.ppermute(a, axis, [(i + 1, i) for i in range(lax.axis_size(axis) - 1)])  1.03 us
    pallas_call x1, Pallas kernels, body(): pl.pallas_call(unpack_kernel, out_shape=jax.ShapeDtypeStruct((8, 64, 448)...  0.86 us
  transfers between devices with their start and end apart: 3, of which 1 were waited for; matrix products, arithmetic and copies ran while one was open for 0% of the time, Pallas kernels for 3%

profile of v3, /device:TPU:56, one launch (start us, length us, event | category | flops | bytes accessed | tf_op | source)
XLA Modules:
  0.0 38.3 jit_solution(14532742265215131134)
XLA Ops:
  0.0 0.0 copy-start
  0.0 3.4 %smooth.1 = (bf16[768,128]{1,0:T(8,128)(2,1)S(1)}, bf16[12,128,128]{2,1,0:T(8,128)(2,1)S(1)}, bf16[384,128]{1,0:T(8,128)(2,1)S(1)}, bf16[384,128]{1,0:T(8,128)(2,1)S(1)}, bf16[816,128]{1,0:T(8,128)(2,1)S(1)}) custom-call(bf16[768,128]{1,0:T(8,128)(2,1)} %bitcast.27, bf16[12,448,128]{2,1,0:T(8,128)(2,1)} %bitcast.20, bf16[24,64]{1,0:T(8,128)(2,1)} %bitcast.28, ...), custom_call_target="tpu_custom_call" | custom-call | tf_op jit(solution)/shard_map/smooth/pallas_call | solution.py:327
  3.4 1.3 %collective-permute-start = (bf16[816,128]{1,0:T(8,128)(2,1)S(1)}, bf16[816,128]{1,0:T(8,128)(2,1)S(1)}, u32[]{:S(2)}, u32[]{:S(2)}) collective-permute-start(bf16[816,128]{1,0:T(8,128)(2,1)S(1)} %get-tuple-element.14), channel_id=1, source_target_pairs={{1,0},{2,1},{3,2},{5,4},{6,5},{7,6},{9,8},{10,9},{11,10},{13,12},{... | collective-permute-start | bytes 626696 | tf_op jit(solution)/shard_map/ppermute | solution.py:350
  4.7 1.9 %collective-permute-start.1 = (bf16[384,128]{1,0:T(8,128)(2,1)S(1)}, bf16[384,128]{1,0:T(8,128)(2,1)S(1)}, u32[]{:S(2)}, u32[]{:S(2)}) collective-permute-start(bf16[384,128]{1,0:T(8,128)(2,1)S(1)} %get-tuple-element.17), channel_id=1, source_target_pairs={{0,4},{4,8},{8,12},{12,16},{16,20},{20,24},{24,28},{28,32},{32,36}... | collective-permute-start | bytes 294920 | tf_op jit(solution)/shard_map/ppermute | solution.py:349
  6.6 14.8 %collective-permute-start.2 = (bf16[384,128]{1,0:T(8,128)(2,1)S(1)}, bf16[384,128]{1,0:T(8,128)(2,1)S(1)}, u32[]{:S(2)}, u32[]{:S(2)}) collective-permute-start(bf16[384,128]{1,0:T(8,128)(2,1)S(1)} %get-tuple-element.18), channel_id=1, source_target_pairs={{4,0},{8,4},{12,8},{16,12},{20,16},{24,20},{28,24},{32,28},{36,32}... | collective-permute-start | bytes 294920 | tf_op jit(solution)/shard_map/ppermute | solution.py:350
  21.4 0.0 collective-permute-done.side_ref
  21.4 0.0 copy-done
  21.4 0.0 copy-start.1
  21.5 1.1 %local_blocks.1 = (bf16[3,192,128]{2,1,0:T(8,128)(2,1)S(1)}, bf16[8,32,128]{2,1,0:T(8,128)(2,1)S(1)}) custom-call(bf16[12,448,128]{2,1,0:T(8,128)(2,1)S(1)} %bitcast.21, bf16[768,128]{1,0:T(8,128)(2,1)S(1)} %get-tuple-element.12.smooth_ref, bf16[12,128,128]{2,1,0:T(8,128)(2,1)S(1)} %get-tuple-element.13.twice_ref, ...), custom_call_target="tpu_custom_call" | custom-call | flops 2000000000 | bytes 3000000 | tf_op jit(solution)/shard_map/local_blocks/pallas_call | solution.py:353
  22.6 0.0 collective-permute-done.1.zlo_ref
  22.6 1.0 %collective-permute-done.2.zhi_ref = bf16[384,128]{1,0:T(8,128)(2,1)S(1)} collective-permute-done((bf16[384,128]{1,0:T(8,128)(2,1)S(1)}, bf16[384,128]{1,0:T(8,128)(2,1)S(1)}, u32[]{:S(2)}, u32[]{:S(2)}) %collective-permute-start.2) | collective-permute-done | bytes 98336 | tf_op jit(solution)/shard_map/ppermute | solution.py:350
  23.6 0.0 copy-done.1
  23.6 1.1 %halo_blocks.1 = bf16[8,224,128]{2,1,0:T(8,128)(2,1)S(1)} custom-call(s32[1,3]{1,0:T(1,128)S(1)} %bitcast.26, bf16[12,448,128]{2,1,0:T(8,128)(2,1)S(1)} %bitcast.22, bf16[768,128]{1,0:T(8,128)(2,1)S(1)} %get-tuple-element.12.smooth_ref, bf16[3,192,128]{2,1,0:T(8,128)(2,1)S(1)} %get-tuple-element.15.part_ref, ...), custom_call_target="tpu_custom_call" | custom-call | tf_op jit(solution)/shard_map/halo_blocks/pallas_call | solution.py:365
  24.7 12.7 %all_to_all.5 = bf16[4,448,128]{2,1,0:T(8,128)(2,1)S(1)} all-to-all(bf16[4,448,128]{2,1,0:T(8,128)(2,1)S(1)} %bitcast.24), channel_id=1, replica_groups=mesh['slab'=192,'col'=4] {'col'}, dimensions={0} | all-to-all | bytes 917504 | tf_op jit(solution)/shard_map/all_to_all | solution.py:373
  37.5 0.9 %unpack.1 = bf16[8,64,448]{2,1,0:T(8,128)(2,1)} custom-call(bf16[8,224,128]{2,1,0:T(8,128)(2,1)S(1)} %bitcast.23), custom_call_target="tpu_custom_call" | custom-call | tf_op jit(solution)/shard_map/unpack/pallas_call | solution.py:374
Async XLA Ops:
  0.0 21.4 %copy-start = (bf16[2,2,6,28672]{3,1,2,0:T(2,128)(2,1)S(1)}, bf16[2,2,6,28672]{3,1,2,0:T(2,128)(2,1)}, u32[]{:S(2)}) copy-start(bf16[2,2,6,28672]{3,1,2,0:T(2,128)(2,1)} %param.5) | copy-start | bytes 4128772
  3.4 18.1 %collective-permute-start = (bf16[816,128]{1,0:T(8,128)(2,1)S(1)}, bf16[816,128]{1,0:T(8,128)(2,1)S(1)}, u32[]{:S(2)}, u32[]{:S(2)}) collective-permute-start(bf16[816,128]{1,0:T(8,128)(2,1)S(1)} %get-tuple-element.14), channel_id=1, source_target_pairs={{1,0},{2,1},{3,2},{5,4},{6,5},{7,6},{9,8},{10,9},{11,10},{13,12},{... | collective-permute-start | bytes 626696 | tf_op jit(solution)/shard_map/ppermute | solution.py:350
  4.7 17.9 %collective-permute-start.1 = (bf16[384,128]{1,0:T(8,128)(2,1)S(1)}, bf16[384,128]{1,0:T(8,128)(2,1)S(1)}, u32[]{:S(2)}, u32[]{:S(2)}) collective-permute-start(bf16[384,128]{1,0:T(8,128)(2,1)S(1)} %get-tuple-element.17), channel_id=1, source_target_pairs={{0,4},{4,8},{8,12},{12,16},{16,20},{20,24},{24,28},{28,32},{32,36}... | collective-permute-start | bytes 294920 | tf_op jit(solution)/shard_map/ppermute | solution.py:349
  6.6 17.0 %collective-permute-start.2 = (bf16[384,128]{1,0:T(8,128)(2,1)S(1)}, bf16[384,128]{1,0:T(8,128)(2,1)S(1)}, u32[]{:S(2)}, u32[]{:S(2)}) collective-permute-start(bf16[384,128]{1,0:T(8,128)(2,1)S(1)} %get-tuple-element.18), channel_id=1, source_target_pairs={{4,0},{8,4},{12,8},{16,12},{20,16},{24,20},{28,24},{32,28},{36,32}... | collective-permute-start | bytes 294920 | tf_op jit(solution)/shard_map/ppermute | solution.py:350
  21.4 2.2 %copy-start.1 = (s32[3,1]{0,1:T(1,128)S(1)}, s32[3,1]{0,1:T(1,128)}, u32[]{:S(2)}) copy-start(s32[3,1]{0,1:T(1,128)} %param.7) | copy-start | bytes 40

commit v4 on v3

--- a/solution.py
+++ b/solution.py
@@ -83,63 +83,50 @@
 
 
 def smooth_kernel(
-    p_hbm, c_hbm, s_hbm, o_hbm, smooth_ref, twice_ref, zlo_ref, zhi_ref, side_ref, p_ref, c_ref, d_ref, s_ref, o_ref, sems
+    p_hbm, c_hbm, s_hbm, o_hbm, smooth_ref, twice_ref, zlo_ref, zhi_ref, side_ref, c_ref, p_ref, s_ref, o_ref, sems
 ):
-    half = LX * 64
-    scaling = pltpu.make_async_copy(s_hbm, s_ref, sems.at[6])
-    naming = pltpu.make_async_copy(o_hbm, o_ref, sems.at[7])
-    scaling.start()
-    layers = []
-    for z in range(LZ):
-        rows, pairs = pl.ds(z * half, half), pl.ds(z * LX, LX)
-        layers.append(
-            (
-                pltpu.make_async_copy(p_hbm.at[rows], p_ref.at[rows], sems.at[3 * z]),
-                pltpu.make_async_copy(c_hbm.at[pairs, 0:64], c_ref.at[pairs], sems.at[3 * z + 1]),
-                pltpu.make_async_copy(c_hbm.at[pairs, 192:256], d_ref.at[pairs], sems.at[3 * z + 2]),
-            )
-        )
-        for copy in layers[z][:2]:
-            copy.start()
-    naming.start()
-    for z in range(LZ):
-        layers[z][2].start()
+    pairs = range(LZ * LX)
+    scaling = pltpu.make_async_copy(s_hbm, s_ref, sems.at[0])
+    reading = pltpu.make_async_copy(p_hbm, p_ref, sems.at[1])
+    naming = pltpu.make_async_copy(o_hbm, o_ref, sems.at[2])
+    first, third, second, last = [
+        pltpu.make_async_copy(c_hbm.at[:, lo:hi], c_ref.at[:, lo:hi], sems.at[3 + n])
+        for n, (lo, hi) in enumerate(((0, 64), (192, 256), (64, 192), (256, 448)))
+    ]
+    for copy in (scaling, reading, first, third, naming, second, last):
+        copy.start()
     matrix = unpairing()
     even = even_rows(64)
     low = low_lanes(32)
     zero = jnp.zeros((64, 128), BF16)
     scaling.wait()
     scale = [scales(s_ref, z) for z in range(LZ)]
-    for z in range(LZ):
-        for copy in layers[z][:2]:
-            copy.wait()
-        at = [z * half + x * 64 for x in range(LX)]
-        tentative = [p_ref[r : r + 64, :] for r in at]
-        twice = doubled(tentative, matrix)
-        right = [jnp.concatenate([diagonal(t[:64]), diagonal(t[64:])], axis=1) for t in twice]
-        both = [jnp.dot(c_ref[z * LX + x], right[x], preferred_element_type=F32) for x in range(LX)]
-        smoothed = [
-            (tentative[x].astype(F32) - scale[z][x * 64 : x * 64 + 64] * pick_y(both[x])).astype(BF16)
-            for x in range(LX)
-        ]
-        twice = doubled(smoothed, matrix)
-        layers[z][2].wait()
-        left = [
-            transposed_dot(jnp.where(even, d_ref[z * LX + x], zero), smoothed[x]) for x in range(LX)
-        ]
-        for x in range(0, LX, 2):
-            to = (z * LX + x) * 32 + LZ * LX * 32
-            side_ref[to : to + 64, :] = combine(left[x], left[x + 1]).astype(BF16)
-        for x in range(LX):
-            smooth_ref[at[x] : at[x] + 64, :] = smoothed[x]
-            twice_ref[z * LX + x] = twice[x]
-            for y in range(2):
-                packed = jnp.where(low, twice[x][y * 64 : y * 64 + 32], twice[x][y * 64 + 32 : y * 64 + 64])
-                to = (x * 2 + y) * 32
-                (zlo_ref, zhi_ref)[z][to : to + 32, :] = packed
-                if y == 0:
-                    to = (z * LX + x) * 32
-                    side_ref[to : to + 32, :] = packed
+    reading.wait()
+    tentative = [p_ref[n * 64 : n * 64 + 64, :] for n in pairs]
+    twice = doubled(tentative, matrix)
+    right = [jnp.concatenate([diagonal(t[:64]), diagonal(t[64:])], axis=1) for t in twice]
+    first.wait()
+    third.wait()
+    both = [jnp.dot(c_ref[n, 0:64, :], right[n], preferred_element_type=F32) for n in pairs]
+    smoothed = [
+        (tentative[n].astype(F32) - scale[n // LX][n % LX * 64 : n % LX * 64 + 64] * pick_y(both[n])).astype(BF16)
+        for n in pairs
+    ]
+    twice = doubled(smoothed, matrix)
+    left = [transposed_dot(jnp.where(even, c_ref[n, 192:256, :], zero), smoothed[n]) for n in pairs]
+    for n in range(0, LZ * LX, 2):
+        to = (n + LZ * LX) * 32
+        side_ref[to : to + 64, :] = combine(left[n], left[n + 1]).astype(BF16)
+    for n in pairs:
+        z, x = n // LX, n % LX
+        smooth_ref[n * 64 : n * 64 + 64, :] = smoothed[n]
+        twice_ref[n] = twice[n]
+        for y in range(2):
+            packed = jnp.where(low, twice[n][y * 64 : y * 64 + 32], twice[n][y * 64 + 32 : y * 64 + 64])
+            to = (x * 2 + y) * 32
+            (zlo_ref, zhi_ref)[z][to : to + 32, :] = packed
+            if y == 0:
+                side_ref[n * 32 : n * 32 + 32, :] = packed
     naming.wait()
     owners = [jnp.broadcast_to(o_ref[:, a : a + 1], (16, 128)) for a in range(LX // 2)]
     for a in range(LX // 2):
@@ -147,6 +134,8 @@
         slot = owners[a] * 2 + rank
         to = 2 * LZ * LX * 32 + a * 16
         side_ref[to : to + 16, :] = slot.astype(F32).astype(BF16)
+    second.wait()
+    last.wait()
 
 
 def combine(even, odd):
@@ -166,7 +155,7 @@
     return lax.dot_general(left, right, (((0,), (0,)), ((), ())), preferred_element_type=F32)
 
 
-def local_kernel(c_ref, smooth_ref, twice_ref, side_ref, part_ref, lent_ref):
+def local_kernel(c_ref, smooth_ref, twice_ref, side_ref, part_ref, lent_ref, turned_ref):
     def both_y(n, swapped=False):
         twice = twice_ref[n]
         first, second = diagonal(twice[:64]), diagonal(twice[64:])
@@ -193,37 +182,25 @@
             above = diagonal_of_packed(side_ref[n * 32 : n * 32 + 32, :])
             product = jnp.dot(block(4), above, preferred_element_type=F32).astype(BF16)
             across[z, x] = jnp.where(even, zero, product)
+    nothing = jnp.zeros((64, 128), BF16)
     for a in range(LX // 2):
-        own = {}
+        turned = []
+        for z in range(LZ):
+            begin = (z * LX + 2 * a) * 64
+            turned.append(smooth_ref[begin : begin + 128, :].T)
+            turned_ref[a, z] = turned[z]
+        right = []
         for z in range(LZ):
             for x in (2 * a, 2 * a + 1):
-                n = z * LX + x
-                own[z, x] = smooth_ref[n * 64 : n * 64 + 64, :]
-        order = [(z, x) for z in range(LZ) for x in (2 * a, 2 * a + 1)]
-        total = transposed_dot(
-            jnp.concatenate([own[k] for k in order], axis=0),
-            jnp.concatenate(
-                [
-                    jnp.concatenate([inner[k] for k in order], axis=0),
-                    jnp.concatenate([across[k] for k in order], axis=0),
-                ],
-                axis=1,
-            ),
+                beside = outer.get((z, x), nothing)
+                ends = [beside, nothing] if x % 2 == 0 else [nothing, beside]
+                right.append(jnp.concatenate([inner[z, x], across[z, x]] + ends, axis=1))
+        total = jnp.dot(
+            jnp.concatenate(turned, axis=1), jnp.concatenate(right, axis=0), preferred_element_type=F32
         )
-        sides = []
-        for x in (2 * a, 2 * a + 1):
-            if (0, x) in outer:
-                sides.append(
-                    transposed_dot(
-                        jnp.concatenate([own[0, x], own[1, x]], axis=0),
-                        jnp.concatenate([outer[0, x], outer[1, x]], axis=0),
-                    )
-                )
-            else:
-                sides.append(jnp.zeros((128, 128), F32))
-        part_ref[a, 0:64, :] = combine(total[:, :128], sides[0]).astype(BF16)
-        part_ref[a, 64:128, :] = to_low(total[:, 128:]).astype(BF16)
-        part_ref[a, 128:192, :] = to_low(sides[1]).astype(BF16)
+        part_ref[a, 0:64, :] = combine(total[:, :128], total[:, 256:384]).astype(BF16)
+        part_ref[a, 64:128, :] = to_low(total[:, 128:256]).astype(BF16)
+        part_ref[a, 128:192, :] = to_low(total[:, 384:]).astype(BF16)
     low = low_lanes(32)
     lent = [jnp.zeros((32, 128), BF16)] * 8
     for a in range(LX // 2):
@@ -249,7 +226,7 @@
         lent_ref[place] = lent[place]
 
 
-def halo_kernel(owner_ref, c_ref, smooth_ref, part_ref, lent_ref, zlo_ref, zhi_ref, out_ref):
+def halo_kernel(owner_ref, c_ref, turned_ref, part_ref, lent_ref, zlo_ref, zhi_ref, out_ref):
     along = {}
     for z in range(LZ):
         for x in range(LX):
@@ -268,11 +245,10 @@
     for a in range(LX // 2):
         ends = [
             to_high(
-                transposed_dot(
-                    jnp.concatenate(
-                        [smooth_ref[(z * LX + x) * 64 : (z * LX + x) * 64 + 64, :] for x in (2 * a, 2 * a + 1)], axis=0
-                    ),
+                jnp.dot(
+                    turned_ref[a, z],
                     jnp.concatenate([along[z, 2 * a], along[z, 2 * a + 1]], axis=0),
+                    preferred_element_type=F32,
                 )
             ).astype(BF16)
             for z in range(LZ)
@@ -324,7 +300,7 @@
     face = jax.ShapeDtypeStruct((LX * 2 * 32, 128), BF16)
     params = pltpu.CompilerParams(vmem_limit_bytes=40 * 2**20)
     arguments = (tentative, blocks, scale, names)
-    smoothed, twice, zlo, zhi, side = pl.pallas_call(
+    smoothed, twice, zlo, zhi, side, held = pl.pallas_call(
         smooth_kernel,
         out_shape=(
             jax.ShapeDtypeStruct((LZ * LX * 64, 128), BF16),
@@ -332,16 +308,15 @@
             face,
             face,
             jax.ShapeDtypeStruct((2 * LZ * LX * 32 + 16 * (LX // 2), 128), BF16),
+            jax.ShapeDtypeStruct((LZ * LX, 448, 128), BF16),
         ),
         in_specs=[pl.BlockSpec(memory_space=pltpu.HBM)] * 4,
-        out_specs=tuple(vmem(5)),
+        out_specs=tuple(vmem(6)),
         scratch_shapes=[
             pltpu.VMEM((LZ * LX * 64, 128), BF16),
-            pltpu.VMEM((LZ * LX, 64, 128), BF16),
-            pltpu.VMEM((LZ * LX, 64, 128), BF16),
             pltpu.VMEM((LZ * LX * 2, 64), BF16),
             pltpu.VMEM((1, LX // 2), jnp.int32),
-            pltpu.SemaphoreType.DMA((8,)),
+            pltpu.SemaphoreType.DMA((7,)),
         ],
         compiler_params=params,
         name="smooth",
@@ -350,18 +325,19 @@
     down = lambda a, axis: lax.ppermute(a, axis, [(i + 1, i) for i in range(lax.axis_size(axis) - 1)])
     from_zlo, from_zhi = up(zhi, "slab"), down(zlo, "slab")
     from_above = down(side, "col")
-    part, lent = pl.pallas_call(
+    part, lent, turned = pl.pallas_call(
         local_kernel,
         out_shape=(
             jax.ShapeDtypeStruct((LX // 2, 192, 128), BF16),
             jax.ShapeDtypeStruct((8, 32, 128), BF16),
+            jax.ShapeDtypeStruct((LX // 2, LZ, 128, 128), BF16),
         ),
         in_specs=vmem(4),
-        out_specs=tuple(vmem(2)),
+        out_specs=tuple(vmem(3)),
         compiler_params=params,
         cost_estimate=pl.CostEstimate(flops=2 * 10**9, bytes_accessed=3 * 10**6, transcendentals=0),
         name="local_blocks",
-    )(blocks, smoothed, twice, from_above)
+    )(held, smoothed, twice, from_above)
     outgoing = pl.pallas_call(
         halo_kernel,
         out_shape=jax.ShapeDtypeStruct((8, 224, 128), BF16),
@@ -369,7 +345,7 @@
         out_specs=vmem(1)[0],
         compiler_params=params,
         name="halo_blocks",
-    )(names, blocks, smoothed, part, lent, from_zlo, from_zhi)
+    )(names, held, turned, part, lent, from_zlo, from_zhi)
     incoming = lax.all_to_all(outgoing.reshape(4, 448, 128), "col", split_axis=0, concat_axis=0, tiled=True)
     return pl.pallas_call(
         unpack_kernel,

time: 38.5 us -> 37.4 us (0.971)
  Pallas kernels: 6.45 us -> 5.26 us
    pallas_call x1, Pallas kernels: 3.37 us -> 2.19 us  [body(): pl.pallas_call(smooth_kernel, out_shape=(jax.ShapeDtypeStruct((LZ * LX *...]
where the time goes in v4:
time: 37.4 us; the launch traced here: 37.1 us
  starting transfers between devices  18 us (48%)
  blocking collectives  12.7 us (34%)
  Pallas kernels  5.26 us (14%)
  waiting for transfers between devices  1.05 us (3%)
    ppermute x2, starting transfers between devices, body(): lax.ppermute(a, axis, [(i + 1, i) for i in range(lax.axis_size(axis) - 1)])  16.1 us
    all_to_all x1, blocking collectives, body(): lax.all_to_all(outgoing.reshape(4, 448, 128), 'col', split_axis=0, concat...  12.7 us
    pallas_call x1, Pallas kernels, body(): pl.pallas_call(smooth_kernel, out_shape=(jax.ShapeDtypeStruct((LZ * LX *...  2.19 us
    ppermute x1, starting transfers between devices, body(): lax.ppermute(a, axis, [(i, i + 1) for i in range(lax.axis_size(axis) - 1)])  1.92 us
    pallas_call x1, Pallas kernels, body(): pl.pallas_call(halo_kernel, out_shape=jax.ShapeDtypeStruct((8, 224, 128),...  1.11 us
    pallas_call x1, Pallas kernels, body(): pl.pallas_call(local_kernel, out_shape=(jax.ShapeDtypeStruct((LX // 2, 19...  1.11 us
    ppermute x2, waiting for transfers between devices, body(): lax.ppermute(a, axis, [(i + 1, i) for i in range(lax.axis_size(axis) - 1)])  1.05 us
    pallas_call x1, Pallas kernels, body(): pl.pallas_call(unpack_kernel, out_shape=jax.ShapeDtypeStruct((8, 64, 448)...  0.86 us
  transfers between devices with their start and end apart: 3, of which 1 were waited for; matrix products, arithmetic and copies ran while one was open for 0% of the time, Pallas kernels for 3%

profile of v4, /device:TPU:56, one launch (start us, length us, event | category | flops | bytes accessed | tf_op | source)
XLA Modules:
  0.0 37.1 jit_solution(2460389089117972145)
XLA Ops:
  0.0 2.2 %smooth.1 = (bf16[768,128]{1,0:T(8,128)(2,1)S(1)}, bf16[12,128,128]{2,1,0:T(8,128)(2,1)S(1)}, bf16[384,128]{1,0:T(8,128)(2,1)S(1)}, bf16[384,128]{1,0:T(8,128)(2...) custom-call(bf16[768,128]{1,0:T(8,128)(2,1)} %bitcast.25, bf16[12,448,128]{2,1,0:T(8,128)(2,1)} %bitcast.24, ...), custom_call_target="tpu_custom_call" | custom-call | tf_op jit(solution)/shard_map/smooth/pallas_call | solution.py:303
  2.2 1.3 %collective-permute-start = (bf16[816,128]{1,0:T(8,128)(2,1)S(1)}, bf16[816,128]{1,0:T(8,128)(2,1)S(1)}, u32[]{:S(2)}, u32[]{:S(2)}) collective-permute-start(bf16[816,128]{1,0:T(8,128)(2,1)S(1)} %get-tuple-element.17), channel_id=1, source_target_pairs={{1,0},{2,1},{3,2},{5,4},{6,5},{7,6},{9,8},{10,9},{11,10},{13,12},{... | collective-permute-start | bytes 626696 | tf_op jit(solution)/shard_map/ppermute | solution.py:325
  3.5 1.9 %collective-permute-start.1 = (bf16[384,128]{1,0:T(8,128)(2,1)S(1)}, bf16[384,128]{1,0:T(8,128)(2,1)S(1)}, u32[]{:S(2)}, u32[]{:S(2)}) collective-permute-start(bf16[384,128]{1,0:T(8,128)(2,1)S(1)} %get-tuple-element.21), channel_id=1, source_target_pairs={{0,4},{4,8},{8,12},{12,16},{16,20},{20,24},{24,28},{28,32},{32,36}... | collective-permute-start | bytes 294920 | tf_op jit(solution)/shard_map/ppermute | solution.py:324
  5.4 14.8 %collective-permute-start.2 = (bf16[384,128]{1,0:T(8,128)(2,1)S(1)}, bf16[384,128]{1,0:T(8,128)(2,1)S(1)}, u32[]{:S(2)}, u32[]{:S(2)}) collective-permute-start(bf16[384,128]{1,0:T(8,128)(2,1)S(1)} %get-tuple-element.22), channel_id=1, source_target_pairs={{4,0},{8,4},{12,8},{16,12},{20,16},{24,20},{28,24},{32,28},{36,32}... | collective-permute-start | bytes 294920 | tf_op jit(solution)/shard_map/ppermute | solution.py:325
  20.2 0.0 collective-permute-done.side_ref
  20.3 0.0 copy-start
  20.3 1.1 %local_blocks.1 = (bf16[3,192,128]{2,1,0:T(8,128)(2,1)S(1)}, bf16[8,32,128]{2,1,0:T(8,128)(2,1)S(1)}, bf16[3,2,128,128]{3,2,1,0:T(8,128)(2,1)S(1)}) custom-call(bf16[12,448,128]{2,1,0:T(8,128)(2,1)S(1)} %get-tuple-element.14.c_ref, bf16[768,128]{1,0:T(8,128)(2,1)S(1)} %get-tuple-element.15.smooth_ref, bf16[12,128,128]{2,1,0:T(8,128)(2,1)S(1)} %get-tuple-element.16.twice_ref, ...), custom_call_target="tpu_custom_call" | custom-call | flops 2000000000 | bytes 3000000 | tf_op jit(solution)/shard_map/local_blocks/pallas_call | solution.py:328
  21.4 0.0 collective-permute-done.1.zlo_ref
  21.4 1.0 %collective-permute-done.2.zhi_ref = bf16[384,128]{1,0:T(8,128)(2,1)S(1)} collective-permute-done((bf16[384,128]{1,0:T(8,128)(2,1)S(1)}, bf16[384,128]{1,0:T(8,128)(2,1)S(1)}, u32[]{:S(2)}, u32[]{:S(2)}) %collective-permute-start.2) | collective-permute-done | bytes 98336 | tf_op jit(solution)/shard_map/ppermute | solution.py:325
  22.4 0.0 copy-done
  22.4 1.1 %halo_blocks.1 = bf16[8,224,128]{2,1,0:T(8,128)(2,1)S(1)} custom-call(s32[1,3]{1,0:T(1,128)S(1)} %bitcast.23, bf16[12,448,128]{2,1,0:T(8,128)(2,1)S(1)} %get-tuple-element.14.c_ref, bf16[3,2,128,128]{3,2,1,0:T(8,128)(2,1)S(1)} %get-tuple-element.18.turned_ref, bf16[3,192,128]{2,1,0:T(8,128)(2,1)S(1)} %get-tuple-element.19.part_ref, ...), custom_call_target="tpu_custom_call" | custom-call | tf_op jit(solution)/shard_map/halo_blocks/pallas_call | solution.py:341
  23.6 12.7 %all_to_all.5 = bf16[4,448,128]{2,1,0:T(8,128)(2,1)S(1)} all-to-all(bf16[4,448,128]{2,1,0:T(8,128)(2,1)S(1)} %bitcast.21), channel_id=1, replica_groups=mesh['slab'=192,'col'=4] {'col'}, dimensions={0} | all-to-all | bytes 917504 | tf_op jit(solution)/shard_map/all_to_all | solution.py:349
  36.3 0.9 %unpack.1 = bf16[8,64,448]{2,1,0:T(8,128)(2,1)} custom-call(bf16[8,224,128]{2,1,0:T(8,128)(2,1)S(1)} %bitcast.20), custom_call_target="tpu_custom_call" | custom-call | tf_op jit(solution)/shard_map/unpack/pallas_call | solution.py:350
Async XLA Ops:
  2.2 18.1 %collective-permute-start = (bf16[816,128]{1,0:T(8,128)(2,1)S(1)}, bf16[816,128]{1,0:T(8,128)(2,1)S(1)}, u32[]{:S(2)}, u32[]{:S(2)}) collective-permute-start(bf16[816,128]{1,0:T(8,128)(2,1)S(1)} %get-tuple-element.17), channel_id=1, source_target_pairs={{1,0},{2,1},{3,2},{5,4},{6,5},{7,6},{9,8},{10,9},{11,10},{13,12},{... | collective-permute-start | bytes 626696 | tf_op jit(solution)/shard_map/ppermute | solution.py:325
  3.5 17.9 %collective-permute-start.1 = (bf16[384,128]{1,0:T(8,128)(2,1)S(1)}, bf16[384,128]{1,0:T(8,128)(2,1)S(1)}, u32[]{:S(2)}, u32[]{:S(2)}) collective-permute-start(bf16[384,128]{1,0:T(8,128)(2,1)S(1)} %get-tuple-element.21), channel_id=1, source_target_pairs={{0,4},{4,8},{8,12},{12,16},{16,20},{20,24},{24,28},{28,32},{32,36}... | collective-permute-start | bytes 294920 | tf_op jit(solution)/shard_map/ppermute | solution.py:324
  5.4 17.0 %collective-permute-start.2 = (bf16[384,128]{1,0:T(8,128)(2,1)S(1)}, bf16[384,128]{1,0:T(8,128)(2,1)S(1)}, u32[]{:S(2)}, u32[]{:S(2)}) collective-permute-start(bf16[384,128]{1,0:T(8,128)(2,1)S(1)} %get-tuple-element.22), channel_id=1, source_target_pairs={{4,0},{8,4},{12,8},{16,12},{20,16},{24,20},{28,24},{32,28},{36,32}... | collective-permute-start | bytes 294920 | tf_op jit(solution)/shard_map/ppermute | solution.py:325
  20.3 2.2 %copy-start = (s32[3,1]{0,1:T(1,128)S(1)}, s32[3,1]{0,1:T(1,128)}, u32[]{:S(2)}) copy-start(s32[3,1]{0,1:T(1,128)} %param.7) | copy-start | bytes 40

commit v5 on v4

--- a/solution.py
+++ b/solution.py
@@ -155,7 +155,18 @@
     return lax.dot_general(left, right, (((0,), (0,)), ((), ())), preferred_element_type=F32)
 
 
-def local_kernel(c_ref, smooth_ref, twice_ref, side_ref, part_ref, lent_ref, turned_ref):
+def along_z(z, halo_ref, c_ref, turned, a):
+    products = []
+    for x in (2 * a, 2 * a + 1):
+        right = jnp.concatenate(
+            [diagonal_of_packed(halo_ref[(x * 2 + y) * 32 : (x * 2 + y) * 32 + 32, :]) for y in range(2)], axis=1
+        )
+        block = c_ref[z * LX + x, (5 + z) * 64 : (6 + z) * 64, :]
+        products.append(pick_y(jnp.dot(block, right, preferred_element_type=F32)).astype(BF16))
+    return to_high(jnp.dot(turned, jnp.concatenate(products, axis=0), preferred_element_type=F32))
+
+
+def local_kernel(c_ref, smooth_ref, twice_ref, side_ref, zlo_ref, part_ref, lent_ref, turned_ref):
     def both_y(n, swapped=False):
         twice = twice_ref[n]
         first, second = diagonal(twice[:64]), diagonal(twice[64:])
@@ -199,7 +210,8 @@
             jnp.concatenate(turned, axis=1), jnp.concatenate(right, axis=0), preferred_element_type=F32
         )
         part_ref[a, 0:64, :] = combine(total[:, :128], total[:, 256:384]).astype(BF16)
-        part_ref[a, 64:128, :] = to_low(total[:, 128:256]).astype(BF16)
+        beyond = along_z(0, zlo_ref, c_ref, turned[0], a)
+        part_ref[a, 64:128, :] = jnp.where(low_lanes(64), to_low(total[:, 128:256]), beyond).astype(BF16)
         part_ref[a, 128:192, :] = to_low(total[:, 384:]).astype(BF16)
     low = low_lanes(32)
     lent = [jnp.zeros((32, 128), BF16)] * 8
@@ -226,38 +238,25 @@
         lent_ref[place] = lent[place]
 
 
-def halo_kernel(owner_ref, c_ref, turned_ref, part_ref, lent_ref, zlo_ref, zhi_ref, out_ref):
-    along = {}
-    for z in range(LZ):
-        for x in range(LX):
-            n = z * LX + x
-            ref = (zlo_ref, zhi_ref)[z]
-            right = jnp.concatenate(
-                [diagonal_of_packed(ref[(x * 2 + y) * 32 : (x * 2 + y) * 32 + 32, :]) for y in range(2)], axis=1
-            )
-            block = c_ref[n, (5 + z) * 64 : (6 + z) * 64, :]
-            along[z, x] = pick_y(jnp.dot(block, right, preferred_element_type=F32)).astype(BF16)
+def halo_kernel(c_ref, turned_ref, part_ref, lent_ref, own_ref, zhi_ref, out_ref):
     low = low_lanes(64)
-    owners = [owner_ref[0, a] for a in range(LX // 2)]
+    begin = 2 * LZ * LX * 32
+    slots = [own_ref[begin + a * 16 : begin + a * 16 + 16, :].astype(F32) for a in range(LX // 2)]
+    here = [[jnp.where(slot == place, 1.0, 0.0).astype(BF16) for slot in slots] for place in range(8)]
+
+    def placed(blocks, place):
+        count = blocks[0].shape[0] // 16
+        masks = [jnp.concatenate([mask] * count, axis=0) for mask in here[place]]
+        return sum([masks[a] * blocks[a] for a in range(1, LX // 2)], masks[0] * blocks[0])
+
+    last = [along_z(1, zhi_ref, c_ref, turned_ref[a, 1], a).astype(BF16) for a in range(LX // 2)]
+    ready = [part_ref[a, 0:128, :] for a in range(LX // 2)]
     for place in range(8):
-        out_ref[place, 0:192, :] = jnp.zeros((192, 128), BF16)
+        out_ref[place, 0:128, :] = placed(ready, place)
         out_ref[place, 192:224, :] = lent_ref[place]
-    for a in range(LX // 2):
-        ends = [
-            to_high(
-                jnp.dot(
-                    turned_ref[a, z],
-                    jnp.concatenate([along[z, 2 * a], along[z, 2 * a + 1]], axis=0),
-                    preferred_element_type=F32,
-                )
-            ).astype(BF16)
-            for z in range(LZ)
-        ]
-        rank = sum([(owners[b] == owners[a]).astype(jnp.int32) for b in range(a)], jnp.int32(0))
-        slot = owners[a] * 2 + rank
-        out_ref[slot, 0:64, :] = part_ref[a, 0:64, :]
-        out_ref[slot, 64:128, :] = jnp.where(low, part_ref[a, 64:128, :], ends[0])
-        out_ref[slot, 128:192, :] = jnp.where(low, part_ref[a, 128:192, :], ends[1])
+    pair = [jnp.where(low, part_ref[a, 128:192, :], last[a]) for a in range(LX // 2)]
+    for place in range(8):
+        out_ref[place, 128:192, :] = placed(pair, place)
 
 
 def unpack_kernel(in_ref, out_hbm, middle_ref, last_ref, sems):
@@ -332,20 +331,20 @@
             jax.ShapeDtypeStruct((8, 32, 128), BF16),
             jax.ShapeDtypeStruct((LX // 2, LZ, 128, 128), BF16),
         ),
-        in_specs=vmem(4),
+        in_specs=vmem(5),
         out_specs=tuple(vmem(3)),
         compiler_params=params,
         cost_estimate=pl.CostEstimate(flops=2 * 10**9, bytes_accessed=3 * 10**6, transcendentals=0),
         name="local_blocks",
-    )(held, smoothed, twice, from_above)
+    )(held, smoothed, twice, from_above, from_zlo)
     outgoing = pl.pallas_call(
         halo_kernel,
         out_shape=jax.ShapeDtypeStruct((8, 224, 128), BF16),
-        in_specs=[pl.BlockSpec(memory_space=pltpu.SMEM)] + vmem(6),
+        in_specs=vmem(6),
         out_specs=vmem(1)[0],
         compiler_params=params,
         name="halo_blocks",
-    )(names, held, turned, part, lent, from_zlo, from_zhi)
+    )(held, turned, part, lent, side, from_zhi)
     incoming = lax.all_to_all(outgoing.reshape(4, 448, 128), "col", split_axis=0, concat_axis=0, tiled=True)
     return pl.pallas_call(
         unpack_kernel,

time: 37.4 us -> 37 us (0.989)
  waiting for transfers between devices: 1.05 us -> 0.59 us
    ppermute x2, waiting for transfers between devices: 1.05 us -> 0.23 us  [body(): lax.ppermute(a, axis, [(i + 1, i) for i in range(lax.axis_size(axis) - 1)])]
    pallas_call x1, Pallas kernels: 1.11 us -> 1.59 us  [body(): pl.pallas_call(local_kernel, out_shape=(jax.ShapeDtypeStruct((LX // 2, 19...]
  transfers between devices with their start and end apart: 3 -> 3, of which waited for: 1 -> 2; matrix products, arithmetic and copies ran while one was open for 0% -> 0% of each run, Pallas kernels for 3% -> 4%
where the time goes in v5:
time: 37 us; the launch traced here: 36.8 us
  starting transfers between devices  18 us (49%)
  blocking collectives  12.7 us (34%)
  Pallas kernels  5.38 us (15%)
  waiting for transfers between devices  0.59 us (2%)
    ppermute x2, starting transfers between devices, body(): lax.ppermute(a, axis, [(i + 1, i) for i in range(lax.axis_size(axis) - 1)])  16.1 us
    all_to_all x1, blocking collectives, body(): lax.all_to_all(outgoing.reshape(4, 448, 128), 'col', split_axis=0, concat...  12.7 us
    pallas_call x1, Pallas kernels, body(): pl.pallas_call(smooth_kernel, out_shape=(jax.ShapeDtypeStruct((LZ * LX *...  2.19 us
    ppermute x1, starting transfers between devices, body(): lax.ppermute(a, axis, [(i, i + 1) for i in range(lax.axis_size(axis) - 1)])  1.92 us
    pallas_call x1, Pallas kernels, body(): pl.pallas_call(local_kernel, out_shape=(jax.ShapeDtypeStruct((LX // 2, 19...  1.59 us
    pallas_call x1, Pallas kernels, body(): pl.pallas_call(unpack_kernel, out_shape=jax.ShapeDtypeStruct((8, 64, 448)...  0.86 us
    pallas_call x1, Pallas kernels, body(): pl.pallas_call(halo_kernel, out_shape=jax.ShapeDtypeStruct((8, 224, 128),...  0.74 us
  transfers between devices with their start and end apart: 3, of which 2 were waited for; matrix products, arithmetic and copies ran while one was open for 0% of the time, Pallas kernels for 4%

profile of v5, /device:TPU:56, one launch (start us, length us, event | category | flops | bytes accessed | tf_op | source)
XLA Modules:
  0.0 36.8 jit_solution(18216027735247390254)
XLA Ops:
  0.0 2.2 %smooth.1 = (bf16[768,128]{1,0:T(8,128)(2,1)S(1)}, bf16[12,128,128]{2,1,0:T(8,128)(2,1)S(1)}, bf16[384,128]{1,0:T(8,128)(2,1)S(1)}, bf16[384,128]{1,0:T(8,128)(2...) custom-call(bf16[768,128]{1,0:T(8,128)(2,1)} %bitcast.23, bf16[12,448,128]{2,1,0:T(8,128)(2,1)} %bitcast.22, ...), custom_call_target="tpu_custom_call" | custom-call | tf_op jit(solution)/shard_map/smooth/pallas_call | solution.py:302
  2.2 1.3 %collective-permute-start = (bf16[816,128]{1,0:T(8,128)(2,1)S(1)}, bf16[816,128]{1,0:T(8,128)(2,1)S(1)}, u32[]{:S(2)}, u32[]{:S(2)}) collective-permute-start(bf16[816,128]{1,0:T(8,128)(2,1)S(1)} %get-tuple-element.17.own_ref), channel_id=1, source_target_pairs={{1,0},{2,1},{3,2},{5,4},{6,5},{7,6},{9,8},{10,9},{11,10},{13,12},{... | collective-permute-start | bytes 626696 | tf_op jit(solution)/shard_map/ppermute | solution.py:324
  3.5 1.9 %collective-permute-start.1 = (bf16[384,128]{1,0:T(8,128)(2,1)S(1)}, bf16[384,128]{1,0:T(8,128)(2,1)S(1)}, u32[]{:S(2)}, u32[]{:S(2)}) collective-permute-start(bf16[384,128]{1,0:T(8,128)(2,1)S(1)} %get-tuple-element.18), channel_id=1, source_target_pairs={{0,4},{4,8},{8,12},{12,16},{16,20},{20,24},{24,28},{28,32},{32,36}... | collective-permute-start | bytes 294920 | tf_op jit(solution)/shard_map/ppermute | solution.py:323
  5.4 14.8 %collective-permute-start.2 = (bf16[384,128]{1,0:T(8,128)(2,1)S(1)}, bf16[384,128]{1,0:T(8,128)(2,1)S(1)}, u32[]{:S(2)}, u32[]{:S(2)}) collective-permute-start(bf16[384,128]{1,0:T(8,128)(2,1)S(1)} %get-tuple-element.22), channel_id=1, source_target_pairs={{4,0},{8,4},{12,8},{16,12},{20,16},{24,20},{28,24},{32,28},{36,32}... | collective-permute-start | bytes 294920 | tf_op jit(solution)/shard_map/ppermute | solution.py:324
  20.2 0.4 collective-permute-done.1.zlo_ref
  20.6 0.0 collective-permute-done.side_ref
  20.6 1.6 %local_blocks.1 = (bf16[3,192,128]{2,1,0:T(8,128)(2,1)S(1)}, bf16[8,32,128]{2,1,0:T(8,128)(2,1)S(1)}, bf16[3,2,128,128]{3,2,1,0:T(8,128)(2,1)S(1)}) custom-call(bf16[12,448,128]{2,1,0:T(8,128)(2,1)S(1)} %get-tuple-element.14.c_ref, bf16[768,128]{1,0:T(8,128)(2,1)S(1)} %get-tuple-element.15.smooth_ref, bf16[12,128,128]{2,1,0:T(8,128)(2,1)S(1)} %get-tuple-element.16.twice_ref, ...), custom_call_target="tpu_custom_call" | custom-call | flops 2000000000 | bytes 3000000 | tf_op jit(solution)/shard_map/local_blocks/pallas_call | solution.py:327
  22.2 0.2 collective-permute-done.2.zhi_ref
  22.4 0.7 %halo_blocks.1 = bf16[8,224,128]{2,1,0:T(8,128)(2,1)S(1)} custom-call(bf16[12,448,128]{2,1,0:T(8,128)(2,1)S(1)} %get-tuple-element.14.c_ref, bf16[3,2,128,128]{3,2,1,0:T(8,128)(2,1)S(1)} %get-tuple-element.19.turned_ref, bf16[3,192,128]{2,1,0:T(8,128)(2,1)S(1)} %get-tuple-element.20.part_ref, bf16[8,32,128]{2,1,0:T(8,128)(2,1)S(1)} %get-tuple-element.21.lent_ref, ...), custom_call_target="tpu_custom_call" | custom-call | tf_op jit(solution)/shard_map/halo_blocks/pallas_call | solution.py:340
  23.2 12.7 %all_to_all.5 = bf16[4,448,128]{2,1,0:T(8,128)(2,1)S(1)} all-to-all(bf16[4,448,128]{2,1,0:T(8,128)(2,1)S(1)} %bitcast.20), channel_id=1, replica_groups=mesh['slab'=192,'col'=4] {'col'}, dimensions={0} | all-to-all | bytes 917504 | tf_op jit(solution)/shard_map/all_to_all | solution.py:348
  35.9 0.9 %unpack.1 = bf16[8,64,448]{2,1,0:T(8,128)(2,1)} custom-call(bf16[8,224,128]{2,1,0:T(8,128)(2,1)S(1)} %bitcast.21), custom_call_target="tpu_custom_call" | custom-call | tf_op jit(solution)/shard_map/unpack/pallas_call | solution.py:349
Async XLA Ops:
  2.2 18.4 %collective-permute-start = (bf16[816,128]{1,0:T(8,128)(2,1)S(1)}, bf16[816,128]{1,0:T(8,128)(2,1)S(1)}, u32[]{:S(2)}, u32[]{:S(2)}) collective-permute-start(bf16[816,128]{1,0:T(8,128)(2,1)S(1)} %get-tuple-element.17.own_ref), channel_id=1, source_target_pairs={{1,0},{2,1},{3,2},{5,4},{6,5},{7,6},{9,8},{10,9},{11,10},{13,12},{... | collective-permute-start | bytes 626696 | tf_op jit(solution)/shard_map/ppermute | solution.py:324
  3.5 17.1 %collective-permute-start.1 = (bf16[384,128]{1,0:T(8,128)(2,1)S(1)}, bf16[384,128]{1,0:T(8,128)(2,1)S(1)}, u32[]{:S(2)}, u32[]{:S(2)}) collective-permute-start(bf16[384,128]{1,0:T(8,128)(2,1)S(1)} %get-tuple-element.18), channel_id=1, source_target_pairs={{0,4},{4,8},{8,12},{12,16},{16,20},{20,24},{24,28},{28,32},{32,36}... | collective-permute-start | bytes 294920 | tf_op jit(solution)/shard_map/ppermute | solution.py:323
  5.4 17.0 %collective-permute-start.2 = (bf16[384,128]{1,0:T(8,128)(2,1)S(1)}, bf16[384,128]{1,0:T(8,128)(2,1)S(1)}, u32[]{:S(2)}, u32[]{:S(2)}) collective-permute-start(bf16[384,128]{1,0:T(8,128)(2,1)S(1)} %get-tuple-element.22), channel_id=1, source_target_pairs={{4,0},{8,4},{12,8},{16,12},{20,16},{24,20},{28,24},{32,28},{36,32}... | collective-permute-start | bytes 294920 | tf_op jit(solution)/shard_map/ppermute | solution.py:324

commit v6 on v5

--- a/solution.py
+++ b/solution.py
@@ -101,19 +101,18 @@
     zero = jnp.zeros((64, 128), BF16)
     scaling.wait()
     scale = [scales(s_ref, z) for z in range(LZ)]
-    reading.wait()
+    for copy in (reading, first, third, naming):
+        copy.wait()
     tentative = [p_ref[n * 64 : n * 64 + 64, :] for n in pairs]
     twice = doubled(tentative, matrix)
     right = [jnp.concatenate([diagonal(t[:64]), diagonal(t[64:])], axis=1) for t in twice]
-    first.wait()
-    third.wait()
     both = [jnp.dot(c_ref[n, 0:64, :], right[n], preferred_element_type=F32) for n in pairs]
     smoothed = [
         (tentative[n].astype(F32) - scale[n // LX][n % LX * 64 : n % LX * 64 + 64] * pick_y(both[n])).astype(BF16)
         for n in pairs
     ]
+    left = [transposed_dot(jnp.where(even, c_ref[n, 192:256, :], zero), smoothed[n]) for n in pairs]
     twice = doubled(smoothed, matrix)
-    left = [transposed_dot(jnp.where(even, c_ref[n, 192:256, :], zero), smoothed[n]) for n in pairs]
     for n in range(0, LZ * LX, 2):
         to = (n + LZ * LX) * 32
         side_ref[to : to + 64, :] = combine(left[n], left[n + 1]).astype(BF16)
@@ -127,7 +126,6 @@
             (zlo_ref, zhi_ref)[z][to : to + 32, :] = packed
             if y == 0:
                 side_ref[n * 32 : n * 32 + 32, :] = packed
-    naming.wait()
     owners = [jnp.broadcast_to(o_ref[:, a : a + 1], (16, 128)) for a in range(LX // 2)]
     for a in range(LX // 2):
         rank = sum([jnp.where(owners[b] == owners[a], 1, 0) for b in range(a)], jnp.zeros((16, 128), jnp.int32))
@@ -267,16 +265,17 @@
     for copy in copies:
         copy.start()
     low = low_lanes(32)
+    pairs = [in_ref[slot, 128:192, :] for slot in range(8)]
     for slot in range(8):
-        pair = in_ref[slot, 128:192, :]
+        last_ref[slot] = pairs[slot][:, 64:]
+    copies.append(pltpu.make_async_copy(last_ref, out_hbm.at[:, :, 384:448], sems.at[2]))
+    copies[2].start()
+    for slot in range(8):
         lent = in_ref[(slot + 6) % 8, 192:224, :]
-        middle_ref[slot, :32, :] = jnp.where(low, pair[:32], swap_halves(lent))
-        middle_ref[slot, 32:, :] = jnp.where(low, pair[32:], lent)
-        last_ref[slot] = pair[:, 64:]
-    copies.append(pltpu.make_async_copy(middle_ref, out_hbm.at[:, :, 128:256], sems.at[2]))
-    copies.append(pltpu.make_async_copy(last_ref, out_hbm.at[:, :, 384:448], sems.at[3]))
-    for copy in copies[2:]:
-        copy.start()
+        middle_ref[slot, :32, :] = jnp.where(low, pairs[slot][:32], swap_halves(lent))
+        middle_ref[slot, 32:, :] = jnp.where(low, pairs[slot][32:], lent)
+    copies.append(pltpu.make_async_copy(middle_ref, out_hbm.at[:, :, 128:256], sems.at[3]))
+    copies[3].start()
     for copy in copies:
         copy.wait()
 

time: 37 us -> 36.9 us (level)
  no operation moved by 1% of the time
where the time goes in v6:
time: 36.9 us; the launch traced here: 36.6 us
  starting transfers between devices  18 us (49%)
  blocking collectives  12.7 us (34%)
  Pallas kernels  5.21 us (14%)
  waiting for transfers between devices  0.59 us (2%)
    ppermute x2, starting transfers between devices, body(): lax.ppermute(a, axis, [(i + 1, i) for i in range(lax.axis_size(axis) - 1)])  16.1 us
    all_to_all x1, blocking collectives, body(): lax.all_to_all(outgoing.reshape(4, 448, 128), 'col', split_axis=0, concat...  12.7 us
    pallas_call x1, Pallas kernels, body(): pl.pallas_call(smooth_kernel, out_shape=(jax.ShapeDtypeStruct((LZ * LX *...  1.98 us
    ppermute x1, starting transfers between devices, body(): lax.ppermute(a, axis, [(i, i + 1) for i in range(lax.axis_size(axis) - 1)])  1.92 us
    pallas_call x1, Pallas kernels, body(): pl.pallas_call(local_kernel, out_shape=(jax.ShapeDtypeStruct((LX // 2, 19...  1.59 us
    pallas_call x1, Pallas kernels, body(): pl.pallas_call(unpack_kernel, out_shape=jax.ShapeDtypeStruct((8, 64, 448)...  0.89 us
    pallas_call x1, Pallas kernels, body(): pl.pallas_call(halo_kernel, out_shape=jax.ShapeDtypeStruct((8, 224, 128),...  0.74 us
  transfers between devices with their start and end apart: 3, of which 2 were waited for; matrix products, arithmetic and copies ran while one was open for 0% of the time, Pallas kernels for 4%

profile of v6, /device:TPU:56, one launch (start us, length us, event | category | flops | bytes accessed | tf_op | source)
XLA Modules:
  0.0 36.6 jit_solution(6384458177551002530)
XLA Ops:
  0.0 2.0 %smooth.1 = (bf16[768,128]{1,0:T(8,128)(2,1)S(1)}, bf16[12,128,128]{2,1,0:T(8,128)(2,1)S(1)}, bf16[384,128]{1,0:T(8,128)(2,1)S(1)}, bf16[384,128]{1,0:T(8,128)(2...) custom-call(bf16[768,128]{1,0:T(8,128)(2,1)} %bitcast.23, bf16[12,448,128]{2,1,0:T(8,128)(2,1)} %bitcast.22, ...), custom_call_target="tpu_custom_call" | custom-call | tf_op jit(solution)/shard_map/smooth/pallas_call | solution.py:301
  2.0 1.3 %collective-permute-start = (bf16[816,128]{1,0:T(8,128)(2,1)S(1)}, bf16[816,128]{1,0:T(8,128)(2,1)S(1)}, u32[]{:S(2)}, u32[]{:S(2)}) collective-permute-start(bf16[816,128]{1,0:T(8,128)(2,1)S(1)} %get-tuple-element.17.own_ref), channel_id=1, source_target_pairs={{1,0},{2,1},{3,2},{5,4},{6,5},{7,6},{9,8},{10,9},{11,10},{13,12},{... | collective-permute-start | bytes 626696 | tf_op jit(solution)/shard_map/ppermute | solution.py:323
  3.3 1.9 %collective-permute-start.1 = (bf16[384,128]{1,0:T(8,128)(2,1)S(1)}, bf16[384,128]{1,0:T(8,128)(2,1)S(1)}, u32[]{:S(2)}, u32[]{:S(2)}) collective-permute-start(bf16[384,128]{1,0:T(8,128)(2,1)S(1)} %get-tuple-element.18), channel_id=1, source_target_pairs={{0,4},{4,8},{8,12},{12,16},{16,20},{20,24},{24,28},{28,32},{32,36}... | collective-permute-start | bytes 294920 | tf_op jit(solution)/shard_map/ppermute | solution.py:322
  5.2 14.8 %collective-permute-start.2 = (bf16[384,128]{1,0:T(8,128)(2,1)S(1)}, bf16[384,128]{1,0:T(8,128)(2,1)S(1)}, u32[]{:S(2)}, u32[]{:S(2)}) collective-permute-start(bf16[384,128]{1,0:T(8,128)(2,1)S(1)} %get-tuple-element.22), channel_id=1, source_target_pairs={{4,0},{8,4},{12,8},{16,12},{20,16},{24,20},{28,24},{32,28},{36,32}... | collective-permute-start | bytes 294920 | tf_op jit(solution)/shard_map/ppermute | solution.py:323
  20.0 0.4 collective-permute-done.1.zlo_ref
  20.4 0.0 collective-permute-done.side_ref
  20.4 1.6 %local_blocks.1 = (bf16[3,192,128]{2,1,0:T(8,128)(2,1)S(1)}, bf16[8,32,128]{2,1,0:T(8,128)(2,1)S(1)}, bf16[3,2,128,128]{3,2,1,0:T(8,128)(2,1)S(1)}) custom-call(bf16[12,448,128]{2,1,0:T(8,128)(2,1)S(1)} %get-tuple-element.14.c_ref, bf16[768,128]{1,0:T(8,128)(2,1)S(1)} %get-tuple-element.15.smooth_ref, bf16[12,128,128]{2,1,0:T(8,128)(2,1)S(1)} %get-tuple-element.16.twice_ref, ...), custom_call_target="tpu_custom_call" | custom-call | flops 2000000000 | bytes 3000000 | tf_op jit(solution)/shard_map/local_blocks/pallas_call | solution.py:326
  22.0 0.2 collective-permute-done.2.zhi_ref
  22.2 0.7 %halo_blocks.1 = bf16[8,224,128]{2,1,0:T(8,128)(2,1)S(1)} custom-call(bf16[12,448,128]{2,1,0:T(8,128)(2,1)S(1)} %get-tuple-element.14.c_ref, bf16[3,2,128,128]{3,2,1,0:T(8,128)(2,1)S(1)} %get-tuple-element.19.turned_ref, bf16[3,192,128]{2,1,0:T(8,128)(2,1)S(1)} %get-tuple-element.20.part_ref, bf16[8,32,128]{2,1,0:T(8,128)(2,1)S(1)} %get-tuple-element.21.lent_ref, ...), custom_call_target="tpu_custom_call" | custom-call | tf_op jit(solution)/shard_map/halo_blocks/pallas_call | solution.py:339
  23.0 12.7 %all_to_all.5 = bf16[4,448,128]{2,1,0:T(8,128)(2,1)S(1)} all-to-all(bf16[4,448,128]{2,1,0:T(8,128)(2,1)S(1)} %bitcast.20), channel_id=1, replica_groups=mesh['slab'=192,'col'=4] {'col'}, dimensions={0} | all-to-all | bytes 917504 | tf_op jit(solution)/shard_map/all_to_all | solution.py:347
  35.7 0.9 %unpack.1 = bf16[8,64,448]{2,1,0:T(8,128)(2,1)} custom-call(bf16[8,224,128]{2,1,0:T(8,128)(2,1)S(1)} %bitcast.21), custom_call_target="tpu_custom_call" | custom-call | tf_op jit(solution)/shard_map/unpack/pallas_call | solution.py:348
Async XLA Ops:
  2.0 18.4 %collective-permute-start = (bf16[816,128]{1,0:T(8,128)(2,1)S(1)}, bf16[816,128]{1,0:T(8,128)(2,1)S(1)}, u32[]{:S(2)}, u32[]{:S(2)}) collective-permute-start(bf16[816,128]{1,0:T(8,128)(2,1)S(1)} %get-tuple-element.17.own_ref), channel_id=1, source_target_pairs={{1,0},{2,1},{3,2},{5,4},{6,5},{7,6},{9,8},{10,9},{11,10},{13,12},{... | collective-permute-start | bytes 626696 | tf_op jit(solution)/shard_map/ppermute | solution.py:323
  3.3 17.1 %collective-permute-start.1 = (bf16[384,128]{1,0:T(8,128)(2,1)S(1)}, bf16[384,128]{1,0:T(8,128)(2,1)S(1)}, u32[]{:S(2)}, u32[]{:S(2)}) collective-permute-start(bf16[384,128]{1,0:T(8,128)(2,1)S(1)} %get-tuple-element.18), channel_id=1, source_target_pairs={{0,4},{4,8},{8,12},{12,16},{16,20},{20,24},{24,28},{28,32},{32,36}... | collective-permute-start | bytes 294920 | tf_op jit(solution)/shard_map/ppermute | solution.py:322
  5.2 17.0 %collective-permute-start.2 = (bf16[384,128]{1,0:T(8,128)(2,1)S(1)}, bf16[384,128]{1,0:T(8,128)(2,1)S(1)}, u32[]{:S(2)}, u32[]{:S(2)}) collective-permute-start(bf16[384,128]{1,0:T(8,128)(2,1)S(1)} %get-tuple-element.22), channel_id=1, source_target_pairs={{4,0},{8,4},{12,8},{16,12},{20,16},{24,20},{28,24},{32,28},{36,32}... | collective-permute-start | bytes 294920 | tf_op jit(solution)/shard_map/ppermute | solution.py:323

commit v7 on v6

--- a/solution.py
+++ b/solution.py
@@ -164,7 +164,18 @@
     return to_high(jnp.dot(turned, jnp.concatenate(products, axis=0), preferred_element_type=F32))
 
 
-def local_kernel(c_ref, smooth_ref, twice_ref, side_ref, zlo_ref, part_ref, lent_ref, turned_ref):
+def places(own_ref):
+    begin = 2 * LZ * LX * 32
+    slots = [own_ref[begin + a * 16 : begin + a * 16 + 16, :].astype(F32) for a in range(LX // 2)]
+    return [[jnp.where(slot == place, 1.0, 0.0).astype(BF16) for slot in slots] for place in range(8)]
+
+
+def placed(blocks, here):
+    masks = [jnp.concatenate([mask] * (blocks[0].shape[0] // 16), axis=0) for mask in here]
+    return sum([masks[a] * blocks[a] for a in range(1, LX // 2)], masks[0] * blocks[0])
+
+
+def local_kernel(c_ref, smooth_ref, twice_ref, side_ref, zlo_ref, own_ref, out_ref, part_ref, turned_ref):
     def both_y(n, swapped=False):
         twice = twice_ref[n]
         first, second = diagonal(twice[:64]), diagonal(twice[64:])
@@ -192,6 +203,7 @@
             product = jnp.dot(block(4), above, preferred_element_type=F32).astype(BF16)
             across[z, x] = jnp.where(even, zero, product)
     nothing = jnp.zeros((64, 128), BF16)
+    ready = []
     for a in range(LX // 2):
         turned = []
         for z in range(LZ):
@@ -207,10 +219,14 @@
         total = jnp.dot(
             jnp.concatenate(turned, axis=1), jnp.concatenate(right, axis=0), preferred_element_type=F32
         )
-        part_ref[a, 0:64, :] = combine(total[:, :128], total[:, 256:384]).astype(BF16)
+        first = combine(total[:, :128], total[:, 256:384]).astype(BF16)
         beyond = along_z(0, zlo_ref, c_ref, turned[0], a)
-        part_ref[a, 64:128, :] = jnp.where(low_lanes(64), to_low(total[:, 128:256]), beyond).astype(BF16)
-        part_ref[a, 128:192, :] = to_low(total[:, 384:]).astype(BF16)
+        second = jnp.where(low_lanes(64), to_low(total[:, 128:256]), beyond).astype(BF16)
+        ready.append(jnp.concatenate([first, second], axis=0))
+        part_ref[a] = to_low(total[:, 384:]).astype(BF16)
+    here = places(own_ref)
+    for place in range(8):
+        out_ref[place, 0:128, :] = placed(ready, here[place])
     low = low_lanes(32)
     lent = [jnp.zeros((32, 128), BF16)] * 8
     for a in range(LX // 2):
@@ -233,28 +249,16 @@
         for place in range(8):
             lent[place] = jnp.where(slot == place, packed.astype(F32), lent[place].astype(F32)).astype(BF16)
     for place in range(8):
-        lent_ref[place] = lent[place]
-
-
-def halo_kernel(c_ref, turned_ref, part_ref, lent_ref, own_ref, zhi_ref, out_ref):
+        out_ref[place, 192:224, :] = lent[place]
+
+
+def halo_kernel(c_ref, turned_ref, part_ref, outgoing_ref, own_ref, zhi_ref, out_ref):
     low = low_lanes(64)
-    begin = 2 * LZ * LX * 32
-    slots = [own_ref[begin + a * 16 : begin + a * 16 + 16, :].astype(F32) for a in range(LX // 2)]
-    here = [[jnp.where(slot == place, 1.0, 0.0).astype(BF16) for slot in slots] for place in range(8)]
-
-    def placed(blocks, place):
-        count = blocks[0].shape[0] // 16
-        masks = [jnp.concatenate([mask] * count, axis=0) for mask in here[place]]
-        return sum([masks[a] * blocks[a] for a in range(1, LX // 2)], masks[0] * blocks[0])
-
+    here = places(own_ref)
     last = [along_z(1, zhi_ref, c_ref, turned_ref[a, 1], a).astype(BF16) for a in range(LX // 2)]
-    ready = [part_ref[a, 0:128, :] for a in range(LX // 2)]
+    pair = [jnp.where(low, part_ref[a], last[a]) for a in range(LX // 2)]
     for place in range(8):
-        out_ref[place, 0:128, :] = placed(ready, place)
-        out_ref[place, 192:224, :] = lent_ref[place]
-    pair = [jnp.where(low, part_ref[a, 128:192, :], last[a]) for a in range(LX // 2)]
-    for place in range(8):
-        out_ref[place, 128:192, :] = placed(pair, place)
+        out_ref[place, 128:192, :] = placed(pair, here[place])
 
 
 def unpack_kernel(in_ref, out_hbm, middle_ref, last_ref, sems):
@@ -323,27 +327,28 @@
     down = lambda a, axis: lax.ppermute(a, axis, [(i + 1, i) for i in range(lax.axis_size(axis) - 1)])
     from_zlo, from_zhi = up(zhi, "slab"), down(zlo, "slab")
     from_above = down(side, "col")
-    part, lent, turned = pl.pallas_call(
+    partial, part, turned = pl.pallas_call(
         local_kernel,
         out_shape=(
-            jax.ShapeDtypeStruct((LX // 2, 192, 128), BF16),
-            jax.ShapeDtypeStruct((8, 32, 128), BF16),
+            jax.ShapeDtypeStruct((8, 224, 128), BF16),
+            jax.ShapeDtypeStruct((LX // 2, 64, 128), BF16),
             jax.ShapeDtypeStruct((LX // 2, LZ, 128, 128), BF16),
         ),
-        in_specs=vmem(5),
+        in_specs=vmem(6),
         out_specs=tuple(vmem(3)),
         compiler_params=params,
         cost_estimate=pl.CostEstimate(flops=2 * 10**9, bytes_accessed=3 * 10**6, transcendentals=0),
         name="local_blocks",
-    )(held, smoothed, twice, from_above, from_zlo)
+    )(held, smoothed, twice, from_above, from_zlo, side)
     outgoing = pl.pallas_call(
         halo_kernel,
         out_shape=jax.ShapeDtypeStruct((8, 224, 128), BF16),
         in_specs=vmem(6),
         out_specs=vmem(1)[0],
+        input_output_aliases={3: 0},
         compiler_params=params,
         name="halo_blocks",
-    )(held, turned, part, lent, side, from_zhi)
+    )(held, turned, part, partial, side, from_zhi)
     incoming = lax.all_to_all(outgoing.reshape(4, 448, 128), "col", split_axis=0, concat_axis=0, tiled=True)
     return pl.pallas_call(
         unpack_kernel,

time: 36.9 us -> 36.9 us (level)
  no operation moved by 1% of the time
where the time goes in v7:
time: 36.9 us; the launch traced here: 36.6 us
  starting transfers between devices  18 us (49%)
  blocking collectives  12.7 us (34%)
  Pallas kernels  5.23 us (14%)
  waiting for transfers between devices  0.57 us (2%)
    ppermute x2, starting transfers between devices, body(): lax.ppermute(a, axis, [(i + 1, i) for i in range(lax.axis_size(axis) - 1)])  16.1 us
    all_to_all x1, blocking collectives, body(): lax.all_to_all(outgoing.reshape(4, 448, 128), 'col', split_axis=0, concat...  12.7 us
    pallas_call x1, Pallas kernels, body(): pl.pallas_call(smooth_kernel, out_shape=(jax.ShapeDtypeStruct((LZ * LX *...  1.99 us
    ppermute x1, starting transfers between devices, body(): lax.ppermute(a, axis, [(i, i + 1) for i in range(lax.axis_size(axis) - 1)])  1.92 us
    pallas_call x1, Pallas kernels, body(): pl.pallas_call(local_kernel, out_shape=(jax.ShapeDtypeStruct((8, 224, 128...  1.61 us
    pallas_call x1, Pallas kernels, body(): pl.pallas_call(unpack_kernel, out_shape=jax.ShapeDtypeStruct((8, 64, 448)...  0.89 us
    pallas_call x1, Pallas kernels, body(): pl.pallas_call(halo_kernel, out_shape=jax.ShapeDtypeStruct((8, 224, 128),...  0.74 us
  transfers between devices with their start and end apart: 3, of which 2 were waited for; matrix products, arithmetic and copies ran while one was open for 0% of the time, Pallas kernels for 4%

profile of v7, /device:TPU:56, one launch (start us, length us, event | category | flops | bytes accessed | tf_op | source)
XLA Modules:
  0.0 36.6 jit_solution(2053692886162827658)
XLA Ops:
  0.0 2.0 %smooth.1 = (bf16[768,128]{1,0:T(8,128)(2,1)S(1)}, bf16[12,128,128]{2,1,0:T(8,128)(2,1)S(1)}, bf16[384,128]{1,0:T(8,128)(2,1)S(1)}, bf16[384,128]{1,0:T(8,128)(2...) custom-call(bf16[768,128]{1,0:T(8,128)(2,1)} %bitcast.23, bf16[12,448,128]{2,1,0:T(8,128)(2,1)} %bitcast.22, ...), custom_call_target="tpu_custom_call" | custom-call | tf_op jit(solution)/shard_map/smooth/pallas_call | solution.py:305
  2.0 1.3 %collective-permute-start = (bf16[816,128]{1,0:T(8,128)(2,1)S(1)}, bf16[816,128]{1,0:T(8,128)(2,1)S(1)}, u32[]{:S(2)}, u32[]{:S(2)}) collective-permute-start(bf16[816,128]{1,0:T(8,128)(2,1)S(1)} %get-tuple-element.17.own_ref), channel_id=1, source_target_pairs={{1,0},{2,1},{3,2},{5,4},{6,5},{7,6},{9,8},{10,9},{11,10},{13,12},{... | collective-permute-start | bytes 626696 | tf_op jit(solution)/shard_map/ppermute | solution.py:327
  3.3 1.9 %collective-permute-start.1 = (bf16[384,128]{1,0:T(8,128)(2,1)S(1)}, bf16[384,128]{1,0:T(8,128)(2,1)S(1)}, u32[]{:S(2)}, u32[]{:S(2)}) collective-permute-start(bf16[384,128]{1,0:T(8,128)(2,1)S(1)} %get-tuple-element.18), channel_id=1, source_target_pairs={{0,4},{4,8},{8,12},{12,16},{16,20},{20,24},{24,28},{28,32},{32,36}... | collective-permute-start | bytes 294920 | tf_op jit(solution)/shard_map/ppermute | solution.py:326
  5.2 14.8 %collective-permute-start.2 = (bf16[384,128]{1,0:T(8,128)(2,1)S(1)}, bf16[384,128]{1,0:T(8,128)(2,1)S(1)}, u32[]{:S(2)}, u32[]{:S(2)}) collective-permute-start(bf16[384,128]{1,0:T(8,128)(2,1)S(1)} %get-tuple-element.22), channel_id=1, source_target_pairs={{4,0},{8,4},{12,8},{16,12},{20,16},{24,20},{28,24},{32,28},{36,32}... | collective-permute-start | bytes 294920 | tf_op jit(solution)/shard_map/ppermute | solution.py:327
  20.0 0.4 collective-permute-done.1.zlo_ref
  20.4 0.0 collective-permute-done.side_ref
  20.4 1.6 %local_blocks.1 = (bf16[8,224,128]{2,1,0:T(8,128)(2,1)S(1)}, bf16[3,64,128]{2,1,0:T(8,128)(2,1)S(1)}, bf16[3,2,128,128]{3,2,1,0:T(8,128)(2,1)S(1)}) custom-call(bf16[12,448,128]{2,1,0:T(8,128)(2,1)S(1)} %get-tuple-element.14.c_ref, bf16[768,128]{1,0:T(8,128)(2,1)S(1)} %get-tuple-element.15.smooth_ref, bf16[12,128,128]{2,1,0:T(8,128)(2,1)S(1)} %get-tuple-element.16.twice_ref, ...), custom_call_target="tpu_custom_call" | custom-call | flops 2000000000 | bytes 3000000 | tf_op jit(solution)/shard_map/local_blocks/pallas_call | solution.py:330
  22.0 0.2 collective-permute-done.2.zhi_ref
  22.2 0.7 %halo_blocks.1 = bf16[8,224,128]{2,1,0:T(8,128)(2,1)S(1)} custom-call(bf16[12,448,128]{2,1,0:T(8,128)(2,1)S(1)} %get-tuple-element.14.c_ref, bf16[3,2,128,128]{3,2,1,0:T(8,128)(2,1)S(1)} %get-tuple-element.19.turned_ref, bf16[3,64,128]{2,1,0:T(8,128)(2,1)S(1)} %get-tuple-element.20.part_ref, ...), custom_call_target="tpu_custom_call", output_to_operand_aliasing={{}: (3, {})} | custom-call | tf_op jit(solution)/shard_map/halo_blocks/pallas_call | solution.py:343
  23.0 12.7 %all_to_all.5 = bf16[4,448,128]{2,1,0:T(8,128)(2,1)S(1)} all-to-all(bf16[4,448,128]{2,1,0:T(8,128)(2,1)S(1)} %bitcast.21), channel_id=1, replica_groups=mesh['slab'=192,'col'=4] {'col'}, dimensions={0} | all-to-all | bytes 917504 | tf_op jit(solution)/shard_map/all_to_all | solution.py:352
  35.7 0.9 %unpack.1 = bf16[8,64,448]{2,1,0:T(8,128)(2,1)} custom-call(bf16[8,224,128]{2,1,0:T(8,128)(2,1)S(1)} %bitcast.20), custom_call_target="tpu_custom_call" | custom-call | tf_op jit(solution)/shard_map/unpack/pallas_call | solution.py:353
Async XLA Ops:
  2.0 18.4 %collective-permute-start = (bf16[816,128]{1,0:T(8,128)(2,1)S(1)}, bf16[816,128]{1,0:T(8,128)(2,1)S(1)}, u32[]{:S(2)}, u32[]{:S(2)}) collective-permute-start(bf16[816,128]{1,0:T(8,128)(2,1)S(1)} %get-tuple-element.17.own_ref), channel_id=1, source_target_pairs={{1,0},{2,1},{3,2},{5,4},{6,5},{7,6},{9,8},{10,9},{11,10},{13,12},{... | collective-permute-start | bytes 626696 | tf_op jit(solution)/shard_map/ppermute | solution.py:327
  3.3 17.1 %collective-permute-start.1 = (bf16[384,128]{1,0:T(8,128)(2,1)S(1)}, bf16[384,128]{1,0:T(8,128)(2,1)S(1)}, u32[]{:S(2)}, u32[]{:S(2)}) collective-permute-start(bf16[384,128]{1,0:T(8,128)(2,1)S(1)} %get-tuple-element.18), channel_id=1, source_target_pairs={{0,4},{4,8},{8,12},{12,16},{16,20},{20,24},{24,28},{28,32},{32,36}... | collective-permute-start | bytes 294920 | tf_op jit(solution)/shard_map/ppermute | solution.py:326
  5.2 17.0 %collective-permute-start.2 = (bf16[384,128]{1,0:T(8,128)(2,1)S(1)}, bf16[384,128]{1,0:T(8,128)(2,1)S(1)}, u32[]{:S(2)}, u32[]{:S(2)}) collective-permute-start(bf16[384,128]{1,0:T(8,128)(2,1)S(1)} %get-tuple-element.22), channel_id=1, source_target_pairs={{4,0},{8,4},{12,8},{16,12},{20,16},{24,20},{28,24},{32,28},{36,32}... | collective-permute-start | bytes 294920 | tf_op jit(solution)/shard_map/ppermute | solution.py:327

commit v8 on v6

--- a/solution.py
+++ b/solution.py
@@ -155,12 +155,15 @@
 
 def along_z(z, halo_ref, c_ref, turned, a):
     products = []
+    even = even_rows(64)
     for x in (2 * a, 2 * a + 1):
         right = jnp.concatenate(
-            [diagonal_of_packed(halo_ref[(x * 2 + y) * 32 : (x * 2 + y) * 32 + 32, :]) for y in range(2)], axis=1
+            [diagonal_of_packed(halo_ref[(x * 2 + y) * 32 : (x * 2 + y) * 32 + 32, :]) for y in range(2)], axis=0
         )
         block = c_ref[z * LX + x, (5 + z) * 64 : (6 + z) * 64, :]
-        products.append(pick_y(jnp.dot(block, right, preferred_element_type=F32)).astype(BF16))
+        zero = jnp.zeros_like(block)
+        left = jnp.concatenate([jnp.where(even, block, zero), jnp.where(even, zero, block)], axis=1)
+        products.append(jnp.dot(left, right, preferred_element_type=F32).astype(BF16))
     return to_high(jnp.dot(turned, jnp.concatenate(products, axis=0), preferred_element_type=F32))
 
 

time: 36.9 us -> 36.9 us (level)
  no operation moved by 1% of the time
where the time goes in v8:
time: 36.9 us; the launch traced here: 36.6 us
  starting transfers between devices  18 us (49%)
  blocking collectives  12.7 us (34%)
  Pallas kernels  5.19 us (14%)
  waiting for transfers between devices  0.61 us (2%)
    ppermute x2, starting transfers between devices, body(): lax.ppermute(a, axis, [(i + 1, i) for i in range(lax.axis_size(axis) - 1)])  16.1 us
    all_to_all x1, blocking collectives, body(): lax.all_to_all(outgoing.reshape(4, 448, 128), 'col', split_axis=0, concat...  12.7 us
    pallas_call x1, Pallas kernels, body(): pl.pallas_call(smooth_kernel, out_shape=(jax.ShapeDtypeStruct((LZ * LX *...  1.98 us
    ppermute x1, starting transfers between devices, body(): lax.ppermute(a, axis, [(i, i + 1) for i in range(lax.axis_size(axis) - 1)])  1.92 us
    pallas_call x1, Pallas kernels, body(): pl.pallas_call(local_kernel, out_shape=(jax.ShapeDtypeStruct((LX // 2, 19...  1.58 us
    pallas_call x1, Pallas kernels, body(): pl.pallas_call(unpack_kernel, out_shape=jax.ShapeDtypeStruct((8, 64, 448)...  0.89 us
    pallas_call x1, Pallas kernels, body(): pl.pallas_call(halo_kernel, out_shape=jax.ShapeDtypeStruct((8, 224, 128),...  0.75 us
  transfers between devices with their start and end apart: 3, of which 2 were waited for; matrix products, arithmetic and copies ran while one was open for 0% of the time, Pallas kernels for 4%

profile of v8, /device:TPU:56, one launch (start us, length us, event | category | flops | bytes accessed | tf_op | source)
XLA Modules:
  0.0 36.6 jit_solution(12573773155178026674)
XLA Ops:
  0.0 2.0 %smooth.1 = (bf16[768,128]{1,0:T(8,128)(2,1)S(1)}, bf16[12,128,128]{2,1,0:T(8,128)(2,1)S(1)}, bf16[384,128]{1,0:T(8,128)(2,1)S(1)}, bf16[384,128]{1,0:T(8,128)(2...) custom-call(bf16[768,128]{1,0:T(8,128)(2,1)} %bitcast.23, bf16[12,448,128]{2,1,0:T(8,128)(2,1)} %bitcast.22, ...), custom_call_target="tpu_custom_call" | custom-call | tf_op jit(solution)/shard_map/smooth/pallas_call | solution.py:304
  2.0 1.3 %collective-permute-start = (bf16[816,128]{1,0:T(8,128)(2,1)S(1)}, bf16[816,128]{1,0:T(8,128)(2,1)S(1)}, u32[]{:S(2)}, u32[]{:S(2)}) collective-permute-start(bf16[816,128]{1,0:T(8,128)(2,1)S(1)} %get-tuple-element.17.own_ref), channel_id=1, source_target_pairs={{1,0},{2,1},{3,2},{5,4},{6,5},{7,6},{9,8},{10,9},{11,10},{13,12},{... | collective-permute-start | bytes 626696 | tf_op jit(solution)/shard_map/ppermute | solution.py:326
  3.3 1.9 %collective-permute-start.1 = (bf16[384,128]{1,0:T(8,128)(2,1)S(1)}, bf16[384,128]{1,0:T(8,128)(2,1)S(1)}, u32[]{:S(2)}, u32[]{:S(2)}) collective-permute-start(bf16[384,128]{1,0:T(8,128)(2,1)S(1)} %get-tuple-element.18), channel_id=1, source_target_pairs={{0,4},{4,8},{8,12},{12,16},{16,20},{20,24},{24,28},{28,32},{32,36}... | collective-permute-start | bytes 294920 | tf_op jit(solution)/shard_map/ppermute | solution.py:325
  5.2 14.8 %collective-permute-start.2 = (bf16[384,128]{1,0:T(8,128)(2,1)S(1)}, bf16[384,128]{1,0:T(8,128)(2,1)S(1)}, u32[]{:S(2)}, u32[]{:S(2)}) collective-permute-start(bf16[384,128]{1,0:T(8,128)(2,1)S(1)} %get-tuple-element.22), channel_id=1, source_target_pairs={{4,0},{8,4},{12,8},{16,12},{20,16},{24,20},{28,24},{32,28},{36,32}... | collective-permute-start | bytes 294920 | tf_op jit(solution)/shard_map/ppermute | solution.py:326
  20.0 0.4 collective-permute-done.1.zlo_ref
  20.4 0.0 collective-permute-done.side_ref
  20.4 1.6 %local_blocks.1 = (bf16[3,192,128]{2,1,0:T(8,128)(2,1)S(1)}, bf16[8,32,128]{2,1,0:T(8,128)(2,1)S(1)}, bf16[3,2,128,128]{3,2,1,0:T(8,128)(2,1)S(1)}) custom-call(bf16[12,448,128]{2,1,0:T(8,128)(2,1)S(1)} %get-tuple-element.14.c_ref, bf16[768,128]{1,0:T(8,128)(2,1)S(1)} %get-tuple-element.15.smooth_ref, bf16[12,128,128]{2,1,0:T(8,128)(2,1)S(1)} %get-tuple-element.16.twice_ref, ...), custom_call_target="tpu_custom_call" | custom-call | flops 2000000000 | bytes 3000000 | tf_op jit(solution)/shard_map/local_blocks/pallas_call | solution.py:329
  22.0 0.2 collective-permute-done.2.zhi_ref
  22.2 0.7 %halo_blocks.1 = bf16[8,224,128]{2,1,0:T(8,128)(2,1)S(1)} custom-call(bf16[12,448,128]{2,1,0:T(8,128)(2,1)S(1)} %get-tuple-element.14.c_ref, bf16[3,2,128,128]{3,2,1,0:T(8,128)(2,1)S(1)} %get-tuple-element.19.turned_ref, bf16[3,192,128]{2,1,0:T(8,128)(2,1)S(1)} %get-tuple-element.20.part_ref, bf16[8,32,128]{2,1,0:T(8,128)(2,1)S(1)} %get-tuple-element.21.lent_ref, ...), custom_call_target="tpu_custom_call" | custom-call | tf_op jit(solution)/shard_map/halo_blocks/pallas_call | solution.py:342
  23.0 12.7 %all_to_all.5 = bf16[4,448,128]{2,1,0:T(8,128)(2,1)S(1)} all-to-all(bf16[4,448,128]{2,1,0:T(8,128)(2,1)S(1)} %bitcast.20), channel_id=1, replica_groups=mesh['slab'=192,'col'=4] {'col'}, dimensions={0} | all-to-all | bytes 917504 | tf_op jit(solution)/shard_map/all_to_all | solution.py:350
  35.7 0.9 %unpack.1 = bf16[8,64,448]{2,1,0:T(8,128)(2,1)} custom-call(bf16[8,224,128]{2,1,0:T(8,128)(2,1)S(1)} %bitcast.21), custom_call_target="tpu_custom_call" | custom-call | tf_op jit(solution)/shard_map/unpack/pallas_call | solution.py:351
Async XLA Ops:
  2.0 18.4 %collective-permute-start = (bf16[816,128]{1,0:T(8,128)(2,1)S(1)}, bf16[816,128]{1,0:T(8,128)(2,1)S(1)}, u32[]{:S(2)}, u32[]{:S(2)}) collective-permute-start(bf16[816,128]{1,0:T(8,128)(2,1)S(1)} %get-tuple-element.17.own_ref), channel_id=1, source_target_pairs={{1,0},{2,1},{3,2},{5,4},{6,5},{7,6},{9,8},{10,9},{11,10},{13,12},{... | collective-permute-start | bytes 626696 | tf_op jit(solution)/shard_map/ppermute | solution.py:326
  3.3 17.1 %collective-permute-start.1 = (bf16[384,128]{1,0:T(8,128)(2,1)S(1)}, bf16[384,128]{1,0:T(8,128)(2,1)S(1)}, u32[]{:S(2)}, u32[]{:S(2)}) collective-permute-start(bf16[384,128]{1,0:T(8,128)(2,1)S(1)} %get-tuple-element.18), channel_id=1, source_target_pairs={{0,4},{4,8},{8,12},{12,16},{16,20},{20,24},{24,28},{28,32},{32,36}... | collective-permute-start | bytes 294920 | tf_op jit(solution)/shard_map/ppermute | solution.py:325
  5.2 17.0 %collective-permute-start.2 = (bf16[384,128]{1,0:T(8,128)(2,1)S(1)}, bf16[384,128]{1,0:T(8,128)(2,1)S(1)}, u32[]{:S(2)}, u32[]{:S(2)}) collective-permute-start(bf16[384,128]{1,0:T(8,128)(2,1)S(1)} %get-tuple-element.22), channel_id=1, source_target_pairs={{4,0},{8,4},{12,8},{16,12},{20,16},{24,20},{28,24},{32,28},{36,32}... | collective-permute-start | bytes 294920 | tf_op jit(solution)/shard_map/ppermute | solution.py:326
